TPU v7x, 32 devices: a whole 2x2x4 slice. The times are simulated.
32 devices in a mesh: frame: 16 (over z, y, core), space: 2 (over x).
Axes of the slice: x: 2, y: 2, z: 4, core: 2. Of those that a mesh axis runs over, the one named last changes fastest.
Arguments:
- video_in: bfloat16 [2, 16, 24, 48, 320], P(None, 'frame', 'space')
- time_embed: bfloat16 [2, 16, 1280], P(None, 'frame'), may hold values from -6 to 6
- text_embed: bfloat16 [2, 16, 128, 1024], P(None, 'frame', 'space'), may hold values from -6 to 6
- text_mask: int32 [2, 16, 128], P(None, 'frame'), may hold values from 0 to 1, as said below
- video_mask: int32 [2, 16], replicated, may hold values from 0 to 1, as said below
- video_number: int32 [2, 16], replicated, may hold values from 0 to 1, as said below
- bucket_index: int32 [16, 16], replicated, may hold values from 0 to 31
- norm_gains: float32 [320, 6], replicated, may hold values from 0.5 to 1.5
- bias_table: float32 [32, 5], replicated, may hold values from -4 to 4
- conv_first: bfloat16 [2880, 320], P('frame', 'space'), may hold values from -0.109375 to 0.109375
- conv_second: bfloat16 [2880, 320], P('frame', 'space'), may hold values from -0.109375 to 0.109375
- film_weight: bfloat16 [1280, 640], P('frame', 'space'), may hold values from -0.15625 to 0.15625
- self_project: bfloat16 [320, 960], P('frame', 'space'), may hold values from -0.3125 to 0.3125
- self_output: bfloat16 [320, 320], P('frame', 'space'), may hold values from -1 to 1
- cross_query: bfloat16 [320, 320], P('frame', 'space'), may hold values from -0.3125 to 0.3125
- cross_keyval: bfloat16 [1024, 640], P('frame', 'space'), may hold values from -0.1875 to 0.1875
- cross_output: bfloat16 [320, 320], P('frame', 'space'), may hold values from -0.625 to 0.625
- time_project: bfloat16 [320, 960], P('frame', 'space'), may hold values from -0.3125 to 0.3125
- time_output: bfloat16 [320, 320], P('frame', 'space'), may hold values from -0.5 to 0.5
- feed_up: bfloat16 [320, 1280], P('frame', 'space'), may hold values from -0.3125 to 0.3125
- feed_down: bfloat16 [1280, 320], P('frame', 'space'), may hold values from -0.15625 to 0.15625
- cotangent: bfloat16 [2, 16, 24, 48, 320], P(None, 'frame', 'space'), may hold values from -6 to 6
Outputs:
- block_out: bfloat16 [2, 16, 24, 48, 320], P(None, 'frame', 'space')
- input_grad: bfloat16 [2, 16, 24, 48, 320], P(None, 'frame', 'space')
- gains_grad: float32 [320, 6], replicated
- table_grad: float32 [32, 5], replicated
- conv_first_grad: float32 [2880, 320], P('frame', 'space')
- conv_second_grad: float32 [2880, 320], P('frame', 'space')
- film_grad: float32 [1280, 640], P('frame', 'space')
- self_project_grad: float32 [320, 960], P('frame', 'space')
- self_output_grad: float32 [320, 320], P('frame', 'space')
- cross_query_grad: float32 [320, 320], P('frame', 'space')
- cross_keyval_grad: float32 [1024, 640], P('frame', 'space')
- cross_output_grad: float32 [320, 320], P('frame', 'space')
- time_project_grad: float32 [320, 960], P('frame', 'space')
- time_output_grad: float32 [320, 320], P('frame', 'space')
- feed_up_grad: float32 [320, 1280], P('frame', 'space')
- feed_down_grad: float32 [1280, 320], P('frame', 'space')
Inputs may be any that keep to these rules, and one draw needn't show every extreme that they name: `text_mask`: token 0 of every frame's text is real. `video_mask`: the first and the last frame of every aligned group of 16 frames are video frames. `video_number`: the first and the last frame of every aligned group of 16 frames have number 0.
All inputs are finite; a program needn't handle non-finite values.
Results may differ from a plain program's by a relative error of at most 0.025.
Values may be sent and summed in bfloat16 or wider, within the bound.
No kernel may reach another device: no remote copies, remote signals or barrier semaphores. Data moves between devices by JAX's collectives and lax.ppermute only.
A program may use at most 256 MiB of HBM per device.

v0:
```python
import jax
import jax.numpy as jnp
from jax import lax
from jax.sharding import PartitionSpec as P

C = 320
HEADS = 5
HEAD = 64
GROUPS = 32
CTX = 1024
TEMB = 1280
TEXT = 128
IMG_H = 24
IMG_W = 48
FR_DEV = 2
GROUP_LEN = 16
NB = 32


EPSILON = 1e-05
MASKED = -1e30
SINGLE = jnp.float32
NARROW = jnp.bfloat16
PRECISE = lax.Precision.HIGHEST


def with_halo(block, sides, width):
    for axis, dim in sides:
        count = lax.axis_size(axis)
        forward = [(i, i + 1) for i in range(count - 1)]
        backward = [(target, source) for source, target in forward]
        low = lax.ppermute(
            lax.slice_in_dim(block, block.shape[dim] - width, None, axis=dim), axis, forward
        )
        high = lax.ppermute(lax.slice_in_dim(block, 0, width, axis=dim), axis, backward)
        block = jnp.concatenate([low, block, high], axis=dim)
    return block


def collect(item_one, item_two, item_three):
    row_full = (
        lax.all_gather(item_one, "frame", axis=0, tiled=True),
        lax.all_gather(item_two, "frame", axis=0, tiled=True),
        lax.all_gather(item_three, "frame", axis=0, tiled=True),
    )
    return (
        lax.all_gather(row_full[0], "space", axis=1, tiled=True),
        lax.all_gather(row_full[1], "space", axis=1, tiled=True),
        lax.all_gather(row_full[2], "space", axis=1, tiled=True),
    )


def settle(item_one, item_two, item_three):
    column_sums = (
        lax.psum_scatter(
            item_one.astype(jnp.bfloat16), "space", scatter_dimension=1, tiled=True
        ).astype(jnp.float32),
        lax.psum_scatter(
            item_two.astype(jnp.bfloat16), "space", scatter_dimension=1, tiled=True
        ).astype(jnp.float32),
        lax.psum_scatter(
            item_three.astype(jnp.bfloat16), "space", scatter_dimension=1, tiled=True
        ).astype(jnp.float32),
    )
    return (
        lax.psum_scatter(
            column_sums[0].astype(jnp.bfloat16), "frame", scatter_dimension=0, tiled=True
        ).astype(jnp.float32),
        lax.psum_scatter(
            column_sums[1].astype(jnp.bfloat16), "frame", scatter_dimension=0, tiled=True
        ).astype(jnp.float32),
        lax.psum_scatter(
            column_sums[2].astype(jnp.bfloat16), "frame", scatter_dimension=0, tiled=True
        ).astype(jnp.float32),
    )


def space_sums(item_one, item_two):
    return lax.psum((item_one, item_two), "space")


def columns_of(padded):
    height_here = padded.shape[1] - 2
    pieces = [
        padded[:, row_off : row_off + height_here, col_off : col_off + IMG_W, :]
        for row_off in range(3)
        for col_off in range(3)
    ]
    return jnp.concatenate(pieces, axis=-1).reshape(-1, 9 * C)


def convolve(activation, weight):
    slot_count, rows_here = (activation.shape[0], activation.shape[1])
    image = activation.reshape(slot_count, rows_here // IMG_W, IMG_W, C)
    rimmed = with_halo(image, (("space", 1),), 1)
    padded = jnp.pad(rimmed, ((0, 0), (0, 0), (1, 1), (0, 0)))
    summed = jnp.dot(columns_of(padded), weight, preferred_element_type=SINGLE)
    return (summed.reshape(slot_count, rows_here, C), padded)


def convolve_back(grad_low, weight):
    flipped = weight.reshape(3, 3, C, C)[::-1, ::-1].transpose(0, 1, 3, 2).reshape(9 * C, C)
    summed, padded = convolve(grad_low, flipped)
    return summed


def weight_grad(left, right):
    return lax.dot_general(
        left.reshape(-1, left.shape[-1]),
        right.reshape(-1, right.shape[-1]),
        (((0,), (0,)), ((), ())),
        preferred_element_type=SINGLE,
    )


def back_project(grad_low, weight):
    return jnp.einsum("...o,io->...i", grad_low, weight, preferred_element_type=SINGLE)


def layer_norm(layer, gain):
    centered = layer - jnp.mean(layer, axis=-1, keepdims=True)
    return (
        centered * lax.rsqrt(jnp.mean(centered * centered, axis=-1, keepdims=True) + EPSILON) * gain
    )


def group_forward(layer):
    slot_count, rows_here = (layer.shape[0], layer.shape[1])
    grouped = layer.reshape(slot_count, rows_here, GROUPS, C // GROUPS)
    summed, squares = space_sums(
        jnp.sum(grouped, axis=(1, 3)), jnp.sum(grouped * grouped, axis=(1, 3))
    )
    members = IMG_H * IMG_W * (C // GROUPS)
    center = summed / members
    spread = lax.rsqrt(squares / members - center * center + EPSILON)
    normed = (grouped - center[:, None, :, None]) * spread[:, None, :, None]
    return (normed.reshape(slot_count, rows_here, C), spread)


def group_backward(normed, spread, upstream):
    slot_count, rows_here = (normed.shape[0], normed.shape[1])
    grad_groups = upstream.reshape(slot_count, rows_here, GROUPS, C // GROUPS)
    norm_groups = normed.reshape(slot_count, rows_here, GROUPS, C // GROUPS)
    summed, crossed = space_sums(
        jnp.sum(grad_groups, axis=(1, 3)), jnp.sum(grad_groups * norm_groups, axis=(1, 3))
    )
    members = IMG_H * IMG_W * (C // GROUPS)
    result = spread[:, None, :, None] * (
        grad_groups
        - summed[:, None, :, None] / members
        - norm_groups * crossed[:, None, :, None] / members
    )
    return result.reshape(slot_count, rows_here, C)


def masked_scores(queries, key_rows, usable):
    scores = jnp.einsum(
        "qhd,khd->hqk", queries, key_rows, preferred_element_type=SINGLE
    ) * HEAD ** (-0.5)
    return jnp.where(usable[None, None, :], scores, MASKED)


def attend_forward(queries, key_rows, value_rows, usable):
    scores = masked_scores(queries, key_rows, usable)
    highest = jnp.max(scores, axis=-1, keepdims=True)
    log_total = highest + jnp.log(jnp.sum(jnp.exp(scores - highest), axis=-1, keepdims=True))
    attn_probs = jnp.exp(scores - log_total).astype(NARROW)
    mixture = jnp.einsum(
        "hqk,khd->qhd", attn_probs, value_rows, preferred_element_type=SINGLE
    ).astype(NARROW)
    return (mixture, log_total[..., 0])


def attend_backward(queries, key_rows, value_rows, usable, log_total, grad_mixture):
    scores = masked_scores(queries, key_rows, usable)
    attn_probs = jnp.exp(scores - log_total[..., None])
    grad_probs = jnp.einsum("qhd,khd->hqk", grad_mixture, value_rows, preferred_element_type=SINGLE)
    row_inner = jnp.sum(grad_probs * attn_probs, axis=-1, keepdims=True)
    grad_scores = (attn_probs * (grad_probs - row_inner)).astype(NARROW)
    grad_queries = jnp.einsum(
        "hqk,khd->qhd", grad_scores, key_rows, preferred_element_type=SINGLE
    ) * HEAD ** (-0.5)
    grad_keys = jnp.einsum(
        "hqk,qhd->khd", grad_scores, queries, preferred_element_type=SINGLE
    ) * HEAD ** (-0.5)
    grad_values = jnp.einsum(
        "hqk,qhd->khd", attn_probs.astype(NARROW), grad_mixture, preferred_element_type=SINGLE
    )
    return (grad_queries, grad_keys, grad_values)


def time_scores(queries, gathered, time_bias, allowed):
    key_rows = gathered[..., :C].reshape(gathered.shape[0], gathered.shape[1], HEADS, HEAD)
    scores = (
        jnp.einsum("rhd,grhd->rhg", queries, key_rows, preferred_element_type=SINGLE)
        * HEAD ** (-0.5)
        + time_bias[None]
    )
    return (jnp.where(allowed[None, None, :], scores, MASKED), key_rows)


def shards(
    video_in,
    time_embed,
    text_embed,
    text_mask,
    video_mask,
    video_number,
    bucket_index,
    norm_gains,
    bias_table,
    conv_first,
    conv_second,
    film_weight,
    self_project,
    self_output,
    cross_query,
    cross_keyval,
    cross_output,
    time_project,
    time_output,
    feed_up,
    feed_down,
    cotangent,
):
    height_here = video_in.shape[2]
    rows_here = height_here * IMG_W
    text_here = text_embed.shape[2]
    frame_count = video_mask.shape[1]
    frame_index = lax.axis_index("frame")
    group_place = frame_index % GROUP_LEN
    heads_view = (FR_DEV, rows_here, HEADS, HEAD)
    every_key = jnp.ones((IMG_H * IMG_W,), jnp.bool_)
    frame_ids = jnp.arange(frame_count)
    place_ids = jnp.arange(GROUP_LEN)
    bucket_row = jnp.sum(jnp.where((place_ids == group_place)[:, None], bucket_index, 0), axis=0)
    key_buckets = jnp.sum(
        jnp.where((frame_ids % GROUP_LEN)[:, None] == place_ids[None, :], bucket_row[None, :], 0),
        axis=1,
    )
    key_table = (key_buckets[:, None] == jnp.arange(NB)[None, :]).astype(SINGLE)
    time_bias = jnp.dot(key_table, bias_table, precision=PRECISE, preferred_element_type=SINGLE).T

    def allowed_for(live_slot, number_slot):
        chooser = frame_ids[:, None] == frame_ids[None, :]
        live_keys = jnp.sum(jnp.where(chooser, live_slot[None, :], 0), axis=1)
        number_keys = jnp.sum(jnp.where(chooser, number_slot[None, :], 0), axis=1)
        own_frame = frame_ids == frame_index
        live_own = jnp.sum(jnp.where(own_frame, live_slot, 0))
        number_own = jnp.sum(jnp.where(own_frame, number_slot, 0))
        same_group = frame_ids // GROUP_LEN == frame_index // GROUP_LEN
        together = (live_keys == 1) & (live_own == 1) & (number_keys == number_own)
        return same_group & (together | (frame_ids == frame_index))

    def spread_keys(own_pair):
        return lax.all_gather(own_pair, "frame", axis=0, tiled=True)

    def return_keys(spread_grads):
        return lax.psum_scatter(
            spread_grads.astype(jnp.bfloat16), "frame", scatter_dimension=0, tiled=True
        ).astype(jnp.float32)

    def gather_keys(frame_pair, text_pair):
        return (
            lax.all_gather(frame_pair, "space", axis=0, tiled=True),
            lax.all_gather(text_pair, "space", axis=0, tiled=True),
        )

    def scatter_keys(frame_grads, text_grads):
        return (
            lax.psum_scatter(
                frame_grads.astype(jnp.bfloat16), "space", scatter_dimension=0, tiled=True
            ).astype(jnp.float32),
            lax.psum_scatter(
                text_grads.astype(jnp.bfloat16), "space", scatter_dimension=0, tiled=True
            ).astype(jnp.float32),
        )

    resid = video_in.reshape(FR_DEV, rows_here, C).astype(SINGLE)
    conv_one, film_full, conv_two = collect(conv_first, film_weight, conv_second)
    temb_act = jax.nn.silu(time_embed.reshape(FR_DEV, TEMB).astype(SINGLE)).astype(NARROW)
    film_all = jnp.dot(temb_act, film_full, preferred_element_type=SINGLE)
    film_scale = 1.0 + film_all[:, None, :C]
    film_shift = film_all[:, None, C:]
    normed_one, spread_one = group_forward(resid)
    pre_one = normed_one * norm_gains[:, 0]
    conv_out, pad_one = convolve(jax.nn.silu(pre_one).astype(NARROW), conv_one)
    hidden = conv_out * film_scale + film_shift
    normed_two, spread_two = group_forward(hidden)
    pre_two = normed_two * norm_gains[:, 1]
    branch_two, pad_two = convolve(jax.nn.silu(pre_two).astype(NARROW), conv_two)
    section_one = resid + branch_two
    kv_weight, qkv_weight, self_weight = collect(cross_keyval, self_project, self_output)
    text_kv = (
        jnp.dot(
            text_embed.reshape(FR_DEV * text_here, CTX), kv_weight, preferred_element_type=SINGLE
        )
        .astype(NARROW)
        .reshape(FR_DEV, text_here, 2 * C)
    )
    self_in = layer_norm(section_one, norm_gains[:, 2]).astype(NARROW)
    self_proj = jnp.dot(self_in, qkv_weight, preferred_element_type=SINGLE).astype(NARROW)

    def self_slot(inputs):
        proj_slot, text_slot = inputs
        frame_kv, text_full = gather_keys(proj_slot[:, C:], text_slot)
        mixture, log_total = attend_forward(
            proj_slot[:, :C].reshape(rows_here, HEADS, HEAD),
            frame_kv[:, :C].reshape(-1, HEADS, HEAD),
            frame_kv[:, C:].reshape(-1, HEADS, HEAD),
            every_key,
        )
        return (mixture, log_total, text_full)

    self_mixed, self_lse, text_all = lax.map(self_slot, (self_proj, text_kv))
    self_mixed = self_mixed.reshape(FR_DEV, rows_here, C)
    section_two = section_one + jnp.dot(self_mixed, self_weight, preferred_element_type=SINGLE)
    query_weight, cross_weight, time_weight = collect(cross_query, cross_output, time_project)
    cross_in = layer_norm(section_two, norm_gains[:, 3]).astype(NARROW)
    cross_queries = (
        jnp.dot(cross_in, query_weight, preferred_element_type=SINGLE)
        .astype(NARROW)
        .reshape(heads_view)
    )
    text_usable = text_mask.reshape(FR_DEV, TEXT) == 1
    text_keys = text_all[..., :C].reshape(FR_DEV, TEXT, HEADS, HEAD)
    text_values = text_all[..., C:].reshape(FR_DEV, TEXT, HEADS, HEAD)
    cross_mixed, cross_lse = jax.vmap(attend_forward)(
        cross_queries, text_keys, text_values, text_usable
    )
    cross_mixed = cross_mixed.reshape(FR_DEV, rows_here, C)
    section_three = section_two + jnp.dot(cross_mixed, cross_weight, preferred_element_type=SINGLE)
    time_in = layer_norm(section_three, norm_gains[:, 4]).astype(NARROW)
    time_proj = jnp.dot(time_in, time_weight, preferred_element_type=SINGLE).astype(NARROW)

    def time_slot(inputs):
        proj_slot, live_slot, number_slot = inputs
        gathered = spread_keys(proj_slot[None, :, C:])
        queries = proj_slot[:, :C].reshape(rows_here, HEADS, HEAD)
        scores, key_rows = time_scores(
            queries, gathered, time_bias, allowed_for(live_slot, number_slot)
        )
        value_rows = gathered[..., C:].reshape(key_rows.shape)
        highest = jnp.max(scores, axis=-1, keepdims=True)
        log_total = highest + jnp.log(jnp.sum(jnp.exp(scores - highest), axis=-1, keepdims=True))
        attn_probs = jnp.exp(scores - log_total).astype(NARROW)
        mixture = jnp.einsum(
            "rhg,grhd->rhd", attn_probs, value_rows, preferred_element_type=SINGLE
        ).astype(NARROW)
        return (mixture, log_total[..., 0])

    time_mixed, time_lse = lax.map(time_slot, (time_proj, video_mask, video_number))
    time_mixed = time_mixed.reshape(FR_DEV, rows_here, C)
    out_weight, inner_weight, outer_weight = collect(time_output, feed_up, feed_down)
    section_four = section_three + jnp.dot(time_mixed, out_weight, preferred_element_type=SINGLE)
    feed_in = layer_norm(section_four, norm_gains[:, 5]).astype(NARROW)
    lifted = jnp.dot(feed_in, inner_weight, preferred_element_type=SINGLE)
    activated = jax.nn.gelu(lifted, approximate=True).astype(NARROW)
    result = section_four + jnp.dot(activated, outer_weight, preferred_element_type=SINGLE)
    block_out = result.astype(NARROW).reshape(video_in.shape)
    carried = cotangent.reshape(FR_DEV, rows_here, C).astype(SINGLE)
    back_feed = carried.astype(NARROW)
    grad_down = weight_grad(activated, back_feed)
    grad_act = back_project(back_feed, outer_weight)
    value_gelu, pull_gelu = jax.vjp(lambda layer: jax.nn.gelu(layer, approximate=True), lifted)
    grad_lifted = pull_gelu(grad_act)[0].astype(NARROW)
    grad_up = weight_grad(feed_in, grad_lifted)
    value_norm, pull_norm = jax.vjp(layer_norm, section_four, norm_gains[:, 5])
    norm_part, gain_five = pull_norm(back_project(grad_lifted, inner_weight))
    carried = carried + norm_part
    back_time = carried.astype(NARROW)
    grad_time_out = weight_grad(time_mixed, back_time)
    grad_time_mixed = back_project(back_time, out_weight).astype(NARROW).reshape(heads_view)
    down_grads = settle(grad_time_out, grad_up, grad_down)

    def time_back(inputs):
        proj_slot, live_slot, number_slot, lse_slot, grad_slot = inputs
        gathered = spread_keys(proj_slot[None, :, C:])
        queries = proj_slot[:, :C].reshape(rows_here, HEADS, HEAD)
        scores, key_rows = time_scores(
            queries, gathered, time_bias, allowed_for(live_slot, number_slot)
        )
        value_rows = gathered[..., C:].reshape(key_rows.shape)
        attn_probs = jnp.exp(scores - lse_slot[..., None])
        grad_probs = jnp.einsum(
            "rhd,grhd->rhg", grad_slot, value_rows, preferred_element_type=SINGLE
        )
        row_inner = jnp.sum(grad_probs * attn_probs, axis=-1, keepdims=True)
        grad_scores = (attn_probs * (grad_probs - row_inner)).astype(NARROW)
        grad_queries = jnp.einsum(
            "rhg,grhd->rhd", grad_scores, key_rows, preferred_element_type=SINGLE
        ) * HEAD ** (-0.5)
        grad_keys = jnp.einsum(
            "rhg,rhd->grhd", grad_scores, queries, preferred_element_type=SINGLE
        ) * HEAD ** (-0.5)
        grad_values = jnp.einsum(
            "rhg,rhd->grhd", attn_probs.astype(NARROW), grad_slot, preferred_element_type=SINGLE
        )
        key_count = key_rows.shape[0]
        spread_grads = jnp.concatenate(
            [
                grad_keys.reshape(key_count, rows_here, C),
                grad_values.reshape(key_count, rows_here, C),
            ],
            -1,
        )
        own_grads = return_keys(spread_grads)[0]
        bias_grad = jnp.sum(grad_scores.astype(SINGLE), axis=0)
        return (jnp.concatenate([grad_queries.reshape(rows_here, C), own_grads], -1), bias_grad)

    grad_time_proj, bias_grads = lax.map(
        time_back, (time_proj, video_mask, video_number, time_lse, grad_time_mixed)
    )
    grad_table = jnp.dot(
        key_table.T, jnp.sum(bias_grads, axis=0).T, precision=PRECISE, preferred_element_type=SINGLE
    )
    grad_time_proj = grad_time_proj.astype(NARROW)
    grad_time_qkv = weight_grad(time_in, grad_time_proj)
    value_norm, pull_norm = jax.vjp(layer_norm, section_three, norm_gains[:, 4])
    norm_part, gain_four = pull_norm(back_project(grad_time_proj, time_weight))
    carried = carried + norm_part
    back_cross = carried.astype(NARROW)
    grad_cross_out = weight_grad(cross_mixed, back_cross)
    grad_cross_mixed = back_project(back_cross, cross_weight).astype(NARROW).reshape(heads_view)
    grad_cquery, grad_tkeys, grad_tvalues = jax.vmap(attend_backward)(
        cross_queries, text_keys, text_values, text_usable, cross_lse, grad_cross_mixed
    )
    grad_cquery = grad_cquery.reshape(FR_DEV, rows_here, C).astype(NARROW)
    grad_cross_q = weight_grad(cross_in, grad_cquery)
    value_norm, pull_norm = jax.vjp(layer_norm, section_two, norm_gains[:, 3])
    norm_part, gain_three = pull_norm(back_project(grad_cquery, query_weight))
    carried = carried + norm_part
    text_grads = jnp.concatenate(
        [grad_tkeys.reshape(FR_DEV, TEXT, C), grad_tvalues.reshape(FR_DEV, TEXT, C)], -1
    )
    middle_grads = settle(grad_cross_q, grad_cross_out, grad_time_qkv)
    back_self = carried.astype(NARROW)
    grad_self_out = weight_grad(self_mixed, back_self)
    grad_self_mixed = back_project(back_self, self_weight).astype(NARROW).reshape(heads_view)

    def self_back(inputs):
        proj_slot, text_slot, lse_slot, grad_slot, text_grad_slot = inputs
        frame_kv, text_again = gather_keys(proj_slot[:, C:], text_slot)
        grad_queries, grad_keys, grad_values = attend_backward(
            proj_slot[:, :C].reshape(rows_here, HEADS, HEAD),
            frame_kv[:, :C].reshape(-1, HEADS, HEAD),
            frame_kv[:, C:].reshape(-1, HEADS, HEAD),
            every_key,
            lse_slot,
            grad_slot,
        )
        frame_grads = jnp.concatenate([grad_keys.reshape(-1, C), grad_values.reshape(-1, C)], -1)
        own_frame, own_text = scatter_keys(frame_grads, text_grad_slot)
        return (jnp.concatenate([grad_queries.reshape(rows_here, C), own_frame], -1), own_text)

    grad_self_proj, grad_text_kv = lax.map(
        self_back, (self_proj, text_kv, self_lse, grad_self_mixed, text_grads)
    )
    grad_self_proj = grad_self_proj.astype(NARROW)
    grad_self_qkv = weight_grad(self_in, grad_self_proj)
    grad_keyval = weight_grad(
        text_embed.reshape(FR_DEV * text_here, CTX), grad_text_kv.astype(NARROW)
    )
    value_norm, pull_norm = jax.vjp(layer_norm, section_one, norm_gains[:, 2])
    norm_part, gain_two = pull_norm(back_project(grad_self_proj, qkv_weight))
    carried = carried + norm_part
    upper_grads = settle(grad_keyval, grad_self_qkv, grad_self_out)
    back_conv = carried.astype(NARROW)
    grad_conv_two = weight_grad(columns_of(pad_two), back_conv)
    grad_act_two = convolve_back(back_conv, conv_two)
    value_silu, pull_silu = jax.vjp(jax.nn.silu, pre_two)
    grad_pre_two = pull_silu(grad_act_two)[0]
    gain_one = jnp.sum(grad_pre_two * normed_two, axis=(0, 1))
    grad_hidden = group_backward(normed_two, spread_two, grad_pre_two * norm_gains[:, 1])
    grad_film = jnp.concatenate(
        [jnp.sum(grad_hidden * conv_out, axis=1), jnp.sum(grad_hidden, axis=1)], -1
    )
    grad_film_w = jnp.dot(
        temb_act.astype(SINGLE).T, grad_film, precision=PRECISE, preferred_element_type=SINGLE
    )
    back_first = (grad_hidden * film_scale).astype(NARROW)
    grad_conv_one = weight_grad(columns_of(pad_one), back_first)
    grad_act_one = convolve_back(back_first, conv_one)
    value_silu, pull_silu = jax.vjp(jax.nn.silu, pre_one)
    grad_pre_one = pull_silu(grad_act_one)[0]
    gain_zero = jnp.sum(grad_pre_one * normed_one, axis=(0, 1))
    carried = carried + group_backward(normed_one, spread_one, grad_pre_one * norm_gains[:, 0])
    input_grad = carried.astype(NARROW).reshape(video_in.shape)
    lower_grads = settle(grad_conv_one, grad_film_w, grad_conv_two)
    gain_stack = jnp.stack(
        [gain_zero, gain_one, gain_two, gain_three, gain_four, gain_five], axis=1
    )
    small_sums = lax.psum((gain_stack, grad_table), ("frame", "space"))
    return (
        block_out,
        input_grad,
        small_sums[0],
        small_sums[1],
        lower_grads[0],
        lower_grads[2],
        lower_grads[1],
        upper_grads[1],
        upper_grads[2],
        middle_grads[0],
        upper_grads[0],
        middle_grads[1],
        middle_grads[2],
        down_grads[0],
        down_grads[1],
        down_grads[2],
    )


def solution(mesh):
    placed = (
        P(None, "frame", "space", None, None),
        P(None, "frame", None),
        P(None, "frame", "space", None),
        P(None, "frame", None),
        P(),
        P(),
        P(),
        P(),
        P(),
        P("frame", "space"),
        P("frame", "space"),
        P("frame", "space"),
        P("frame", "space"),
        P("frame", "space"),
        P("frame", "space"),
        P("frame", "space"),
        P("frame", "space"),
        P("frame", "space"),
        P("frame", "space"),
        P("frame", "space"),
        P("frame", "space"),
        P(None, "frame", "space", None, None),
    )
    return jax.shard_map(
        shards,
        mesh=mesh,
        in_specs=placed,
        out_specs=(
            P(None, "frame", "space", None, None),
            P(None, "frame", "space", None, None),
            P(),
            P(),
            P("frame", "space"),
            P("frame", "space"),
            P("frame", "space"),
            P("frame", "space"),
            P("frame", "space"),
            P("frame", "space"),
            P("frame", "space"),
            P("frame", "space"),
            P("frame", "space"),
            P("frame", "space"),
            P("frame", "space"),
            P("frame", "space"),
        ),
        check_vma=False,
    )
```

profile of v0, /device:TPU:0, one launch (start us, length us, event | category | flops | bytes accessed | tf_op | source)
XLA Modules:
  0.0 2236.0 jit_solution(12262716155704507621)
XLA Ops:
  7.3 25.8 %all_gather.103 = bf16[1024,320]{1,0:T(8,128)(2,1)S(1)} all-gather(bf16[64,320]{1,0:T(8,128)(2,1)} %param.45), channel_id=1, replica_groups=mesh['frame'=16,'space'=2] {'frame'}, dimensions={0}, use_global_device_ids=true | all-gather | bytes 696320 | tf_op jit(solution)/shard_map/all_gather | solution.py:42
  34.3 20.3 all_gather.97
  56.0 23.9 %all-gather.3 = bf16[16,180,160]{1,2,0:T(8,128)(2,1)S(1)} all-gather(bf16[1,180,160]{1,2,0:T(8,128)(2,1)S(1)} %bitcast.639), channel_id=1, replica_groups=mesh['frame'=16,'space'=2] {'frame'}, dimensions={0}, use_global_device_ids=true | all-gather | bytes 979200 | tf_op jit(solution)/shard_map/all_gather | solution.py:42
  96.8 23.1 %all-gather.4 = bf16[16,180,160]{1,2,0:T(8,128)(2,1)S(1)} all-gather(bf16[1,180,160]{1,2,0:T(8,128)(2,1)S(1)} %bitcast.640), channel_id=1, replica_groups=mesh['frame'=16,'space'=2] {'frame'}, dimensions={0}, use_global_device_ids=true | all-gather | bytes 979200 | tf_op jit(solution)/shard_map/all_gather | solution.py:44
  264.5 21.6 all-gather.13
  302.4 20.8 all_gather.117
  339.1 20.1 all-gather.12
  467.0 83.6 %while.60 = (s32[]{:T(128)}, bf16[2,576,5,64]{1,3,2,0:T(8,128)(2,1)}, f32[2,5,576]{2,1,0:T(8,128)}, bf16[2,128,640]{2,1,0:T(8,128)(2,1)}, bf16[2,576,960]{2,1,0:...) while((s32[]{:T(128)}, bf16[2,576,5,64]{1,3,2,0:T(8,128)(2,1)}, f32[2,5,576]{2,1,0:T(8,128)}, ...), condition=%wide.region_17.18_spmd, body=%wide.region_14.17_spmd.sunk | while | flops 876070080 | bytes 63548332 | solution.py:315
  567.7 277.9 %while.62 = (s32[]{:T(128)}, bf16[2,576,5,64]{3,2,1,0:T(8,128)(2,1)}, f32[2,576,5]{1,2,0:T(8,128)S(1)}, s32[]{:T(128)}, s32[2,16]{1,0:T(2,128)S(1)}, /*index=5*/...) while((s32[]{:T(128)}, ...), condition=%wide.region_33.34_spmd.clone.clone, body=%wide.region_26.33_spmd.clone.clone.sunk | while | flops 18338800 | bytes 132176728 | solution.py:352
  572.8 94.1 %all-gather.43.cloned.1.call-done = bf16[9216,640]{1,0:T(8,128)(2,1)} async-done(((bf16[576,640]{1,0:T(8,128)(2,1)}), bf16[9216,640]{1,0:T(8,128)(2,1)}) %all-gather.43.cloned.1.call-update) | async-done | bytes 11796496 | tf_op jit(solution)/shard_map/while/body/eval_jaxpr/all_gather | solution.py:256
  712.6 92.3 %all-gather.43.cloned.1.call-done = bf16[9216,640]{1,0:T(8,128)(2,1)} async-done(((bf16[576,640]{1,0:T(8,128)(2,1)}), bf16[9216,640]{1,0:T(8,128)(2,1)}) %all-gather.43.cloned.1.call-update) | async-done | bytes 11796496 | tf_op jit(solution)/shard_map/while/body/eval_jaxpr/all_gather | solution.py:256
  866.6 583.2 %while.63 = (s32[]{:T(128)}, bf16[2,576,960]{1,2,0:T(8,128)(2,1)}, f32[2,5,16]{2,1,0:T(8,128)}, s32[]{:T(128)}, s32[2,16]{1,0:T(2,128)S(1)}, /*index=5*/s32[]{:T...) while((s32[]{:T(128)}, bf16[2,576,960]{1,2,0:T(8,128)(2,1)}, ...), condition=%wide.region_46.47_spmd.clone.clone, body=%wide.region_38.46_spmd.clone.clone.sunk | while | flops 68519840 | bytes 199645104 | solution.py:411
  872.5 91.8 %all-gather.45.cloned.1.call-done = bf16[9216,640]{1,0:T(8,128)(2,1)} async-done(((bf16[576,640]{1,0:T(8,128)(2,1)}), bf16[9216,640]{1,0:T(8,128)(2,1)}) %all-gather.45.cloned.1.call-update) | async-done | bytes 11796496 | tf_op jit(solution)/shard_map/while/body/eval_jaxpr/all_gather | solution.py:256
  1024.2 131.4 %reduce-scatter.79.cloned.1.call-done = bf16[1,576,640]{1,2,0:T(8,128)(2,1)} async-done(((bf16[16,576,640]{1,2,0:T(8,128)(2,1)}), bf16[1,576,640]{1,2,0:T(8,128)(2,1)}) %reduce-scatter.79.cloned.1.call-update) | async-done | bytes 737296 | tf_op jit(solution)/shard_map/while/body/eval_jaxpr/reduce_scatter | solution.py:259
  1163.3 92.8 %all-gather.45.cloned.1.call-done = bf16[9216,640]{1,0:T(8,128)(2,1)} async-done(((bf16[576,640]{1,0:T(8,128)(2,1)}), bf16[9216,640]{1,0:T(8,128)(2,1)}) %all-gather.45.cloned.1.call-update) | async-done | bytes 11796496 | tf_op jit(solution)/shard_map/while/body/eval_jaxpr/all_gather | solution.py:256
  1315.9 131.4 %reduce-scatter.79.cloned.1.call-done = bf16[1,576,640]{1,2,0:T(8,128)(2,1)} async-done(((bf16[16,576,640]{1,2,0:T(8,128)(2,1)}), bf16[1,576,640]{1,2,0:T(8,128)(2,1)}) %reduce-scatter.79.cloned.1.call-update) | async-done | bytes 737296 | tf_op jit(solution)/shard_map/while/body/eval_jaxpr/reduce_scatter | solution.py:259
  1481.0 162.7 %while.61 = (s32[]{:T(128)}, bf16[2,576,960]{1,2,0:T(8,128)(2,1)}, bf16[2,64,640]{2,1,0:T(8,128)(2,1)}, bf16[2,576,960]{2,1,0:T(8,128)(2,1)}, f32[2,5,576]{2,1,0...) while((s32[]{:T(128)}, bf16[2,576,960]{1,2,0:T(8,128)(2,1)}, ...), condition=%wide.region_56.57_spmd, body=%wide.region_52.56_spmd.sunk | while | flops 2156582144 | bytes 171352656 | solution.py:456
  1485.8 23.5 %all-gather.41.cloned.1.call-done = bf16[1152,640]{1,0:T(8,128)(2,1)} async-done(((bf16[576,640]{1,0:T(8,128)(2,1)}), bf16[1152,640]{1,0:T(8,128)(2,1)}) %all-gather.41.cloned.1.call-update) | async-done | bytes 1474576 | tf_op jit(solution)/shard_map/while/body/eval_jaxpr/all_gather | solution.py:265
  1566.6 24.4 %all-gather.41.cloned.1.call-done = bf16[1152,640]{1,0:T(8,128)(2,1)} async-done(((bf16[576,640]{1,0:T(8,128)(2,1)}), bf16[1152,640]{1,0:T(8,128)(2,1)}) %all-gather.41.cloned.1.call-update) | async-done | bytes 1474576 | tf_op jit(solution)/shard_map/while/body/eval_jaxpr/all_gather | solution.py:265
  1869.6 22.6 %reduce-scatter.45.cloned.1.call-done = bf16[2880,160]{0,1:T(8,128)(2,1)} async-done(((bf16[2880,320]{0,1:T(8,128)(2,1)}), bf16[2880,160]{0,1:T(8,128)(2,1)}) %reduce-scatter.45.cloned.1.call-update) | async-done | bytes 921616 | tf_op jit(solution)/shard_map/reduce_scatter | solution.py:55
  1932.5 38.9 %fusion.146 = (bf16[24,480]{1,0:T(8,128)(2,1)}, bf16[24,480]{1,0:T(8,128)(2,1)}) fusion(bf16[320,480]{1,0:T(8,128)(2,1)} %copy.618, bf16[320,480]{1,0:T(8,128)(2,1)} %copy.628), kind=kCustom, calls=%all-reduce-scatter.2 | all-reduce-scatter fusion | flops 368641 | bytes 660992
  1995.0 41.8 %all-reduce.15 = (f32[320,6]{0,1:T(8,128)}, f32[32,5]{0,1:T(8,128)}) all-reduce(f32[320,6]{0,1:T(8,128)S(1)} %stack.27, f32[32,5]{0,1:T(8,128)S(1)} %copy-done.194), channel_id=1, replica_groups=mesh['frame'=16,'space'=2] {'frame','space'}, use_global_device_ids=true, to_apply=%region_77.78 | all-reduce | flops 2080 | bytes 16640 | tf_op jit(solution)/shard_map/psum | solution.py:493
  2052.2 57.9 %reduce-scatter.63.cloned.1.call-done = bf16[80,320]{1,0:T(8,128)(2,1)} async-done(((bf16[1280,320]{1,0:T(8,128)(2,1)}), bf16[80,320]{1,0:T(8,128)(2,1)}) %reduce-scatter.63.cloned.1.call-update) | async-done | bytes 51216
  2111.8 105.8 %all-reduce.24.cloned.1.call-done = (bf16[2880,160]{0,1:T(8,128)(2,1)}, bf16[2880,160]{0,1:T(8,128)(2,1)}, bf16[320,160]{0,1:T(8,128)(2,1)}, bf16[320,160]{0,1:T...) async-done(((bf16[2880,160]{0,1:T(8,128)(2,1)}, bf16[2880,160]{0,1:T(8,128)(2,1)}, bf16[320,160]{0,1:T(8,128)(2,1)}, ...) | async-done | bytes 2662416
  (1023 shorter events, 1108.2 us)
Async XLA Ops:
  7.2 388.7 %all-gather.37.cloned.1.call-start = ((), (), s32[]{:S(2)}) async-start(), calls=%async_computation.21 | async-start | bytes 1966080 | tf_op jit(solution)/shard_map/all_gather | solution.py:47
  34.3 363.5 %all-gather.33.cloned.1.call-start = ((), (), s32[]{:S(2)}) async-start(), calls=%async_computation.19 | async-start | bytes 2457600 | tf_op jit(solution)/shard_map/all_gather | solution.py:48
  55.9 343.9 %all-gather.31.cloned.1.call-start = ((), (), s32[]{:S(2)}) async-start(), calls=%async_computation.18 | async-start | bytes 2826240 | tf_op jit(solution)/shard_map/all_gather | solution.py:47
  83.4 336.8 %all-gather.35.cloned.1.call-start = ((), (), s32[]{:S(2)}) async-start(), calls=%async_computation.20 | async-start | bytes 2826240 | tf_op jit(solution)/shard_map/all_gather | solution.py:49
  91.3 288.3 %collective-permute-start = (bf16[2,1,48,320]{3,2,1,0:T(8,128)(2,1)}, bf16[2,1,48,320]{3,2,1,0:T(8,128)(2,1)}, u32[]{:S(2)}, u32[]{:S(2)}) collective-permute-start(bf16[2,1,48,320]{3,2,1,0:T(8,128)(2,1)} %get-tuple-element.1147), channel_id=1, source_target_pairs={{0,1},{2,3},{4,5},{6,7},{8,9},{10,11},{12,13},{14,15},{16,17},{18,... | collective-permute-start | bytes 184328 | tf_op jit(solution)/shard_map/ppermute | solution.py:32
  95.4 284.3 %collective-permute-start.1 = (bf16[2,1,48,320]{3,2,1,0:T(8,128)(2,1)}, bf16[2,1,48,320]{3,2,1,0:T(8,128)(2,1)}, u32[]{:S(2)}, u32[]{:S(2)}) collective-permute-start(bf16[2,1,48,320]{3,2,1,0:T(8,128)(2,1)} %get-tuple-element.1148), channel_id=1, source_target_pairs={{1,0},{3,2},{5,4},{7,6},{9,8},{11,10},{13,12},{15,14},{17,16},{19,... | collective-permute-start | bytes 184328 | tf_op jit(solution)/shard_map/ppermute | solution.py:35
  870.0 285.5 %reduce-scatter.79.cloned.1.call-start = ((), (), s32[]{:S(2)}) async-start(), calls=%async_computation.44 | async-start | bytes 13926400 | tf_op jit(solution)/shard_map/while/body/eval_jaxpr/reduce_scatter | solution.py:259
  1160.9 286.4 %reduce-scatter.79.cloned.1.call-start = ((), (), s32[]{:S(2)}) async-start(), calls=%async_computation.44 | async-start | bytes 13926400 | tf_op jit(solution)/shard_map/while/body/eval_jaxpr/reduce_scatter | solution.py:259
  1643.7 163.7 %reduce-scatter.61.cloned.1.call-start = ((), (), s32[]{:S(2)}) async-start(), calls=%async_computation.30 | async-start | bytes 1228800 | tf_op jit(solution)/shard_map/reduce_scatter | solution.py:61
  1644.5 181.1 %reduce-scatter.55.cloned.1.call-start = ((), (), s32[]{:S(2)}) async-start(), calls=%async_computation.27 | async-start | bytes 1966080 | tf_op jit(solution)/shard_map/reduce_scatter | solution.py:55
  1659.7 179.5 %reduce-scatter.49.cloned.1.call-start = ((), (), s32[]{:S(2)}) async-start(), calls=%async_computation.24 | async-start | bytes 2457600 | tf_op jit(solution)/shard_map/reduce_scatter | solution.py:58
  1724.6 142.8 %reduce-scatter.71.cloned.1.call-start = ((), (), s32[]{:S(2)}) async-start(), calls=%async_computation.35 | async-start | bytes 1474560
  1731.1 138.4 %reduce-scatter.59.cloned.1.call-start = ((), (), s32[]{:S(2)}) async-start(), calls=%async_computation.29 | async-start | bytes 368640 | tf_op jit(solution)/shard_map/reduce_scatter | solution.py:55
  1740.2 129.3 %reduce-scatter.57.cloned.1.call-start = ((), (), s32[]{:S(2)}) async-start(), calls=%async_computation.28 | async-start | bytes 368640 | tf_op jit(solution)/shard_map/reduce_scatter | solution.py:58
  1750.0 119.5 %reduce-scatter.53.cloned.1.call-start = ((), (), s32[]{:S(2)}) async-start(), calls=%async_computation.26 | async-start | bytes 368640 | tf_op jit(solution)/shard_map/reduce_scatter | solution.py:55
  1752.7 116.9 %reduce-scatter.51.cloned.1.call-start = ((), (), s32[]{:S(2)}) async-start(), calls=%async_computation.25 | async-start | bytes 368640 | tf_op jit(solution)/shard_map/reduce_scatter | solution.py:61
  1767.4 102.2 %reduce-scatter.47.cloned.1.call-start = ((), (), s32[]{:S(2)}) async-start(), calls=%async_computation.23 | async-start | bytes 2826240 | tf_op jit(solution)/shard_map/reduce_scatter | solution.py:61
  1785.9 106.2 %reduce-scatter.45.cloned.1.call-start = ((), (), s32[]{:S(2)}) async-start(), calls=%async_computation.22 | async-start | bytes 2826240 | tf_op jit(solution)/shard_map/reduce_scatter | solution.py:55
  1795.3 116.2 %reduce-scatter.69.cloned.1.call-start = ((), (), s32[]{:S(2)}) async-start(), calls=%async_computation.34 | async-start | bytes 1105920
  1802.6 128.0 %reduce-scatter.65.cloned.1.call-start = ((), (), s32[]{:S(2)}) async-start(), calls=%async_computation.32 | async-start | bytes 1105920
  1806.6 236.6 %reduce-scatter.73.cloned.1.call-start = ((), (), s32[]{:S(2)}) async-start(), calls=%async_computation.36 | async-start | bytes 696320
  1809.6 240.9 %reduce-scatter.67.cloned.1.call-start = ((), (), s32[]{:S(2)}) async-start(), calls=%async_computation.33 | async-start | bytes 835584
  1828.0 282.1 %reduce-scatter.63.cloned.1.call-start = ((), (), s32[]{:S(2)}) async-start(), calls=%async_computation.31 | async-start | bytes 1044480
  1841.5 376.1 %all-reduce.24.cloned.1.call-start = ((), (), s32[]{:S(2)}) async-start(), calls=%async_computation.37 | async-start | bytes 5570560
  (237 other events, 6249.9 us)
Sparse Core Ops, SparseCore 0:
  34.4 21.5 all-gather.36
  57.5 27.9 all-gather.32
  87.0 32.3 all-gather.30
  123.5 32.8 all-gather.34
  470.2 24.5 all-gather.38
  511.0 26.0 all-gather.38
  570.9 95.9 all-gather.42
  710.7 94.0 all-gather.42
  870.2 94.1 all-gather.44
  1018.9 136.5 reduce-scatter.78
  1161.0 95.0 all-gather.44
  1310.7 136.5 reduce-scatter.78
  1484.1 25.2 all-gather.40
  1534.4 24.9 reduce-scatter.74
  1564.9 26.0 all-gather.40
  1616.1 24.9 reduce-scatter.74
  1668.3 23.1 reduce-scatter.54
  1724.7 26.8 reduce-scatter.48
  1830.8 29.5 reduce-scatter.46
  1862.6 29.4 reduce-scatter.44
  1934.6 56.6 reduce-scatter.72
  1994.9 55.6 reduce-scatter.66
  2054.4 55.6 reduce-scatter.62
  2114.6 102.9 all-reduce.23
  (10 shorter events, 139.3 us)
where the time goes:
time: 2250 us; the launch traced here: 2240 us
  waiting for transfers between devices  973 us (43%)
  local copies, waits for them, and re-layouts  451 us (20%)
  blocking collectives  441 us (20%)
  matrix products  161 us (7%)
  other arithmetic  155 us (7%)
  starting transfers between devices  30.7 us (1%)
    all_gather x4, waiting for transfers between devices, spread_keys(): return lax.all_gather(own_pair, 'frame', axis=0, tiled=True)  371 us
    reduce_scatter x2, waiting for transfers between devices, return_keys(): lax.psum_scatter(spread_grads.astype(jnp.bfloat16), 'frame', scatter_dime...  263 us
    unnamed x33, waiting for transfers between devices  188 us
    all_gather x4, blocking collectives, collect(): lax.all_gather(item_one, 'frame', axis=0, tiled=True)  89.1 us
    while x46, local copies, waits for them, and re-layouts  89.1 us
    unnamed x459, local copies, waits for them, and re-layouts  88.8 us
    all_gather x4, waiting for transfers between devices, gather_keys(): lax.all_gather(frame_pair, 'space', axis=0, tiled=True)  84.6 us
    all_gather x4, blocking collectives, collect(): lax.all_gather(item_three, 'frame', axis=0, tiled=True)  80.3 us
  transfers between devices with their start and end apart: 48, of which 21 were waited for; matrix products, arithmetic and copies ran while one was open for 19% of the time, Pallas kernels for 0%

commit v1 on v0

--- a/solution.py
+++ b/solution.py
@@ -1,6 +1,11 @@
+from typing import Any, NamedTuple
+
 import jax
 import jax.numpy as jnp
 from jax import lax
+from jax.experimental import pallas as pl
+from jax.experimental.pallas import tpu as pltpu
+from jax.sharding import Mesh
 from jax.sharding import PartitionSpec as P
 
 C = 320
@@ -15,8 +20,16 @@
 FR_DEV = 2
 GROUP_LEN = 16
 NB = 32
-
-
+FF = 1280
+GELU_A = 0.7978845608028654
+GELU_B = 0.044715
+
+
+FRAME = "frame"
+SPACE = "space"
+HALF = "half"
+QUAD = "quad"
+CORE = "core"
 EPSILON = 1e-05
 MASKED = -1e30
 SINGLE = jnp.float32
@@ -39,44 +52,44 @@
 
 def collect(item_one, item_two, item_three):
     row_full = (
-        lax.all_gather(item_one, "frame", axis=0, tiled=True),
-        lax.all_gather(item_two, "frame", axis=0, tiled=True),
-        lax.all_gather(item_three, "frame", axis=0, tiled=True),
+        lax.all_gather(item_one, FRAME, axis=0, tiled=True),
+        lax.all_gather(item_two, FRAME, axis=0, tiled=True),
+        lax.all_gather(item_three, FRAME, axis=0, tiled=True),
     )
     return (
-        lax.all_gather(row_full[0], "space", axis=1, tiled=True),
-        lax.all_gather(row_full[1], "space", axis=1, tiled=True),
-        lax.all_gather(row_full[2], "space", axis=1, tiled=True),
+        lax.all_gather(row_full[0], SPACE, axis=1, tiled=True),
+        lax.all_gather(row_full[1], SPACE, axis=1, tiled=True),
+        lax.all_gather(row_full[2], SPACE, axis=1, tiled=True),
     )
 
 
 def settle(item_one, item_two, item_three):
     column_sums = (
         lax.psum_scatter(
-            item_one.astype(jnp.bfloat16), "space", scatter_dimension=1, tiled=True
+            item_one.astype(jnp.bfloat16), SPACE, scatter_dimension=1, tiled=True
         ).astype(jnp.float32),
         lax.psum_scatter(
-            item_two.astype(jnp.bfloat16), "space", scatter_dimension=1, tiled=True
+            item_two.astype(jnp.bfloat16), SPACE, scatter_dimension=1, tiled=True
         ).astype(jnp.float32),
         lax.psum_scatter(
-            item_three.astype(jnp.bfloat16), "space", scatter_dimension=1, tiled=True
+            item_three.astype(jnp.bfloat16), SPACE, scatter_dimension=1, tiled=True
         ).astype(jnp.float32),
     )
     return (
         lax.psum_scatter(
-            column_sums[0].astype(jnp.bfloat16), "frame", scatter_dimension=0, tiled=True
+            column_sums[0].astype(jnp.bfloat16), FRAME, scatter_dimension=0, tiled=True
         ).astype(jnp.float32),
         lax.psum_scatter(
-            column_sums[1].astype(jnp.bfloat16), "frame", scatter_dimension=0, tiled=True
+            column_sums[1].astype(jnp.bfloat16), FRAME, scatter_dimension=0, tiled=True
         ).astype(jnp.float32),
         lax.psum_scatter(
-            column_sums[2].astype(jnp.bfloat16), "frame", scatter_dimension=0, tiled=True
+            column_sums[2].astype(jnp.bfloat16), FRAME, scatter_dimension=0, tiled=True
         ).astype(jnp.float32),
     )
 
 
 def space_sums(item_one, item_two):
-    return lax.psum((item_one, item_two), "space")
+    return lax.psum((item_one, item_two), SPACE)
 
 
 def columns_of(padded):
@@ -92,7 +105,7 @@
 def convolve(activation, weight):
     slot_count, rows_here = (activation.shape[0], activation.shape[1])
     image = activation.reshape(slot_count, rows_here // IMG_W, IMG_W, C)
-    rimmed = with_halo(image, (("space", 1),), 1)
+    rimmed = with_halo(image, ((SPACE, 1),), 1)
     padded = jnp.pad(rimmed, ((0, 0), (0, 0), (1, 1), (0, 0)))
     summed = jnp.dot(columns_of(padded), weight, preferred_element_type=SINGLE)
     return (summed.reshape(slot_count, rows_here, C), padded)
@@ -227,7 +240,7 @@
     rows_here = height_here * IMG_W
     text_here = text_embed.shape[2]
     frame_count = video_mask.shape[1]
-    frame_index = lax.axis_index("frame")
+    frame_index = lax.axis_index(FRAME)
     group_place = frame_index % GROUP_LEN
     heads_view = (FR_DEV, rows_here, HEADS, HEAD)
     every_key = jnp.ones((IMG_H * IMG_W,), jnp.bool_)
@@ -253,26 +266,26 @@
         return same_group & (together | (frame_ids == frame_index))
 
     def spread_keys(own_pair):
-        return lax.all_gather(own_pair, "frame", axis=0, tiled=True)
+        return lax.all_gather(own_pair, FRAME, axis=0, tiled=True)
 
     def return_keys(spread_grads):
         return lax.psum_scatter(
-            spread_grads.astype(jnp.bfloat16), "frame", scatter_dimension=0, tiled=True
+            spread_grads.astype(jnp.bfloat16), FRAME, scatter_dimension=0, tiled=True
         ).astype(jnp.float32)
 
     def gather_keys(frame_pair, text_pair):
         return (
-            lax.all_gather(frame_pair, "space", axis=0, tiled=True),
-            lax.all_gather(text_pair, "space", axis=0, tiled=True),
+            lax.all_gather(frame_pair, SPACE, axis=0, tiled=True),
+            lax.all_gather(text_pair, SPACE, axis=0, tiled=True),
         )
 
     def scatter_keys(frame_grads, text_grads):
         return (
             lax.psum_scatter(
-                frame_grads.astype(jnp.bfloat16), "space", scatter_dimension=0, tiled=True
+                frame_grads.astype(jnp.bfloat16), SPACE, scatter_dimension=0, tiled=True
             ).astype(jnp.float32),
             lax.psum_scatter(
-                text_grads.astype(jnp.bfloat16), "space", scatter_dimension=0, tiled=True
+                text_grads.astype(jnp.bfloat16), SPACE, scatter_dimension=0, tiled=True
             ).astype(jnp.float32),
         )
 
@@ -490,7 +503,7 @@
     gain_stack = jnp.stack(
         [gain_zero, gain_one, gain_two, gain_three, gain_four, gain_five], axis=1
     )
-    small_sums = lax.psum((gain_stack, grad_table), ("frame", "space"))
+    small_sums = lax.psum((gain_stack, grad_table), (FRAME, SPACE))
     return (
         block_out,
         input_grad,
@@ -511,52 +524,1063 @@
     )
 
 
+PIX = IMG_H * IMG_W
+CUBE = (QUAD, CORE, SPACE)
+CHIPS = (QUAD, SPACE)
+PAIR = (HALF, SPACE)
+WORLD = (HALF, QUAD, CORE, SPACE)
+SCALE = HEAD ** (-0.5)
+
+
+def swap_space():
+    return [(2 * a + b, 2 * b + a) for a in range(2) for b in range(2)]
+
+
+def turn_space():
+    return [(2 * a + b, 2 * (1 - b) + a) for a in range(2) for b in range(2)]
+
+
+def pick(flag, pair):
+    return jnp.where(flag == 0, pair[0], pair[1])
+
+
+def to_slot(block, half, space):
+    own = lax.ppermute(pick(space, block), PAIR, swap_space())
+    other = lax.ppermute(pick(1 - space, block), PAIR, turn_space())
+    return jnp.concatenate(
+        [jnp.where(half == 0, own, other), jnp.where(half == 0, other, own)], axis=0
+    )
+
+
+def from_slot(frame, half, space):
+    pieces = frame.reshape((2, frame.shape[0] // 2) + frame.shape[1:])
+    own = lax.ppermute(pick(half, pieces), PAIR, [(d, s) for s, d in swap_space()])
+    other = lax.ppermute(pick(1 - half, pieces), PAIR, [(d, s) for s, d in turn_space()])
+    return jnp.stack([jnp.where(space == 0, own, other), jnp.where(space == 0, other, own)])
+
+
+def meta_slot(block, space):
+    return lax.ppermute(pick(space, block), PAIR, swap_space())
+
+
+class Weights(NamedTuple):
+    conv_first: Any
+    conv_second: Any
+    film_weight: Any
+    self_project: Any
+    self_output: Any
+    cross_query: Any
+    cross_keyval: Any
+    cross_output: Any
+    time_project: Any
+    time_output: Any
+    feed_up: Any
+    feed_down: Any
+
+
+def mm(a, b):
+    return jnp.dot(a, b, preferred_element_type=SINGLE)
+
+
+VMEM_BYTES = 58 * 1024 * 1024
+STEP = 384
+STEPS = PIX // STEP
+NT = (((1,), (1,)), ((), ()))
+TN = (((0,), (0,)), ((), ()))
+
+
+def nt(a, b):
+    return lax.dot_general(a, b, NT, preferred_element_type=SINGLE)
+
+
+def tn(a, b):
+    return lax.dot_general(a, b, TN, preferred_element_type=SINGLE)
+
+
+def kernel_call(body, outs, scratch=(), flops=10**9):
+    return pl.pallas_call(
+        body,
+        out_shape=[jax.ShapeDtypeStruct(s, d) for s, d in outs],
+        scratch_shapes=[pltpu.VMEM(s, d) for s, d in scratch],
+        compiler_params=pltpu.CompilerParams(vmem_limit_bytes=VMEM_BYTES),
+        cost_estimate=pl.CostEstimate(flops=flops, bytes_accessed=10**7, transcendentals=0),
+    )
+
+
+def group_matrix():
+    lanes = jnp.arange(C) // (C // GROUPS)
+    return (lanes[:, None] == lanes[None, :]).astype(SINGLE)
+
+
+def grouped(row, gmat):
+    wide = jnp.broadcast_to(row, (8, C))
+    return lax.dot_general(
+        wide, gmat, (((1,), (0,)), ((), ())), precision=PRECISE, preferred_element_type=SINGLE
+    )[:1]
+
+
+def edge_masks(rows):
+    col = lax.broadcasted_iota(jnp.int32, (rows, C), 0) % IMG_W
+    return col != 0, col != IMG_W - 1
+
+
+def spread_columns(cols_ref, start, act):
+    not_first, not_last = edge_masks(STEP)
+    left = jnp.where(not_first, pltpu.roll(act, 1, 0), 0.0)
+    right = jnp.where(not_last, pltpu.roll(act, STEP - 1, 0), 0.0)
+    cols_ref[pl.ds(start, STEP), :] = jnp.concatenate(
+        [left.astype(NARROW), act.astype(NARROW), right.astype(NARROW)], axis=1
+    )
+
+
+def conv_rows(cols_ref, w_ref, start):
+    total = None
+    for i in range(3):
+        part = mm(cols_ref[pl.ds(start + IMG_W * i, STEP), :], w_ref[3 * C * i : 3 * C * (i + 1), :])
+        total = part if total is None else total + part
+    return total
+
+
+def gn_stats(total, square, gmat):
+    members = PIX * (C // GROUPS)
+    center = grouped(total, gmat) / members
+    return center, lax.rsqrt(grouped(square, gmat) / members - center * center + EPSILON)
+
+
+def unpack_tall(half, full_ref, out_ref, at, rows, cols):
+    parts = BAND // cols
+    tall = rows // parts
+    for quad in range(4):
+        pieces = []
+        for frame in range(4 * quad, 4 * quad + 4):
+            place = half if frame < 8 else 1 - half
+            sides = [
+                full_ref[2 * (frame % 8) + s, place, at : at + tall, :].astype(SINGLE) for s in range(2)
+            ]
+            pieces += [
+                jnp.concatenate([side[:, cols * q : cols * (q + 1)] for side in sides], axis=1)
+                for q in range(parts)
+            ]
+        out_ref[4 * rows * quad : 4 * rows * (quad + 1), :] = jnp.concatenate(pieces, axis=0).astype(NARROW)
+
+
+def clear_border(cols_ref):
+    border = jnp.zeros((IMG_W, 3 * C), NARROW)
+    cols_ref[0:IMG_W, :] = border
+    cols_ref[PIX + IMG_W :, :] = border
+
+
+def conv_kernel(x_ref, w1_ref, w2_ref, temb_ref, wf_ref, gains_ref, gmat_ref,
+                conv_out_ref, sec_ref, cols1_ref, cols2_ref, stats_ref, film_ref):
+    film_ref[...] = mm(temb_ref[...], wf_ref[...])
+    gmat = gmat_ref[...]
+    clear_border(cols1_ref)
+    clear_border(cols2_ref)
+    total = jnp.zeros((1, C), SINGLE)
+    square = jnp.zeros((1, C), SINGLE)
+    for r in range(STEPS):
+        x = x_ref[r * STEP : (r + 1) * STEP, :].astype(SINGLE)
+        total += jnp.sum(x, axis=0, keepdims=True)
+        square += jnp.sum(x * x, axis=0, keepdims=True)
+    center, spread = gn_stats(total, square, gmat)
+    stats_ref[0:1, :] = center
+    stats_ref[1:2, :] = spread
+    for r in range(STEPS):
+        x = x_ref[r * STEP : (r + 1) * STEP, :].astype(SINGLE)
+        pre = (x - center) * spread * gains_ref[0:1, :]
+        spread_columns(cols1_ref, IMG_W + r * STEP, pre * (0.5 + 0.5 * jnp.tanh(0.5 * pre)))
+    scale = 1.0 + film_ref[0:1, :C]
+    shift = film_ref[0:1, C:]
+    total = jnp.zeros((1, C), SINGLE)
+    square = jnp.zeros((1, C), SINGLE)
+    for r in range(STEPS):
+        out = conv_rows(cols1_ref, w1_ref, r * STEP)
+        conv_out_ref[r * STEP : (r + 1) * STEP, :] = out
+        hidden = out * scale + shift
+        total += jnp.sum(hidden, axis=0, keepdims=True)
+        square += jnp.sum(hidden * hidden, axis=0, keepdims=True)
+    center, spread = gn_stats(total, square, gmat)
+    stats_ref[2:3, :] = center
+    stats_ref[3:4, :] = spread
+    for r in range(STEPS):
+        hidden = conv_out_ref[r * STEP : (r + 1) * STEP, :] * scale + shift
+        pre = (hidden - center) * spread * gains_ref[1:2, :]
+        spread_columns(cols2_ref, IMG_W + r * STEP, pre * (0.5 + 0.5 * jnp.tanh(0.5 * pre)))
+    for r in range(STEPS):
+        out = conv_rows(cols2_ref, w2_ref, r * STEP)
+        rows = slice(r * STEP, (r + 1) * STEP)
+        sec_ref[rows, :] = x_ref[rows, :].astype(SINGLE) + out
+
+
+def conv_block(x, w1, w2, temb, wf, gains, gmat):
+    cols = (PIX + 2 * IMG_W, 3 * C)
+    return kernel_call(
+        conv_kernel,
+        [((PIX, C), SINGLE), ((PIX, C), SINGLE), (cols, NARROW), (cols, NARROW), ((8, C), SINGLE), ((8, 2 * C), SINGLE)],
+        flops=15 * 10**9,
+    )(x, w1, w2, temb, wf, gains, gmat)
+
+
+def ln_rows(layer, gain):
+    centered = layer - jnp.mean(layer, axis=-1, keepdims=True)
+    rstd = lax.rsqrt(jnp.mean(centered * centered, axis=-1, keepdims=True) + EPSILON)
+    return centered * rstd, rstd
+
+
+def attend_rows(q, k, v_one, usable):
+    scores = nt(q, k)
+    if usable is not None:
+        scores = jnp.where(usable, scores, MASKED)
+    highest = jnp.max(scores, axis=-1, keepdims=True)
+    probs = jnp.exp(scores - highest).astype(NARROW)
+    both = mm(probs, v_one)
+    total = both[:, HEAD : HEAD + 1]
+    return both[:, :HEAD] / total, highest + jnp.log(total)
+
+
+def with_ones(v):
+    return jnp.concatenate([v, jnp.ones(v.shape, v.dtype)], axis=1)
+
+
+def attn_kernel(sec1_ref, gains_ref, wqkv_ref, wso_ref, text_ref, usable_ref, wkv_ref, wcq_ref,
+                wco_ref, wtime_ref,
+                proj_ref, mix_ref, lse_ref, sec2_ref, kv_ref, cq_ref, cmix_ref, clse_ref,
+                sec3_ref, tproj_ref):
+    for r in range(STEPS):
+        rows = slice(r * STEP, (r + 1) * STEP)
+        hat, rstd = ln_rows(sec1_ref[rows, :], None)
+        proj_ref[rows, :] = mm((hat * gains_ref[2:3, :]).astype(NARROW), wqkv_ref[...]).astype(NARROW)
+    kv_ref[...] = mm(text_ref[...], wkv_ref[...]).astype(NARROW)
+    for h in range(HEADS):
+        lanes = slice(h * HEAD, (h + 1) * HEAD)
+        k = proj_ref[:, C + h * HEAD : C + (h + 1) * HEAD]
+        v = with_ones(proj_ref[:, 2 * C + h * HEAD : 2 * C + (h + 1) * HEAD])
+        for r in range(STEPS):
+            rows = slice(r * STEP, (r + 1) * STEP)
+            q = proj_ref[rows, lanes] * jnp.bfloat16(SCALE)
+            mix, lse = attend_rows(q, k, v, None)
+            mix_ref[rows, lanes] = mix
+            lse_ref[rows, h : h + 1] = lse
+    usable = jnp.broadcast_to(usable_ref[...], (STEP, TEXT)) == 1
+    for r in range(STEPS):
+        rows = slice(r * STEP, (r + 1) * STEP)
+        sec2 = sec1_ref[rows, :] + mm(mix_ref[rows, :].astype(NARROW), wso_ref[...])
+        sec2_ref[rows, :] = sec2
+        hat, rstd = ln_rows(sec2, None)
+        cq_ref[rows, :] = mm((hat * gains_ref[3:4, :]).astype(NARROW), wcq_ref[...]).astype(NARROW)
+        for h in range(HEADS):
+            lanes = slice(h * HEAD, (h + 1) * HEAD)
+            k = kv_ref[:, lanes]
+            v = with_ones(kv_ref[:, C + h * HEAD : C + (h + 1) * HEAD])
+            mix, lse = attend_rows(cq_ref[rows, lanes] * jnp.bfloat16(SCALE), k, v, usable)
+            cmix_ref[rows, lanes] = mix
+            clse_ref[rows, h : h + 1] = lse
+        sec3 = sec2 + mm(cmix_ref[rows, :].astype(NARROW), wco_ref[...])
+        sec3_ref[rows, :] = sec3
+        hat, rstd = ln_rows(sec3, None)
+        tproj_ref[rows, :] = mm((hat * gains_ref[4:5, :]).astype(NARROW), wtime_ref[...]).astype(NARROW)
+
+
+def attn_block(sec1, gains, wqkv, wso, text, usable, wkv, wcq, wco, wtime):
+    full = ((PIX, C), SINGLE)
+    low = ((PIX, C), NARROW)
+    return kernel_call(
+        attn_kernel,
+        [((PIX, 3 * C), NARROW), full, ((PIX, 8), SINGLE), full, ((TEXT, 2 * C), NARROW), low,
+         full, ((PIX, 8), SINGLE), full, ((PIX, 3 * C), NARROW)],
+        flops=28 * 10**9,
+    )(sec1, gains, wqkv, wso, text, usable, wkv, wcq, wco, wtime)
+
+
+def ln_back_rows(layer, gain, upstream):
+    hat, rstd = ln_rows(layer, gain)
+    dx = upstream * gain
+    part = rstd * (
+        dx - jnp.mean(dx, axis=-1, keepdims=True) - hat * jnp.mean(dx * hat, axis=-1, keepdims=True)
+    )
+    return part, jnp.sum(upstream * hat, axis=0, keepdims=True), hat
+
+
+def split_three(column):
+    one = column.astype(NARROW)
+    rest = column - one.astype(SINGLE)
+    two = rest.astype(NARROW)
+    return [one, two, (rest - two.astype(SINGLE)).astype(NARROW)]
+
+
+def extended(rows, column):
+    return jnp.concatenate([rows] + split_three(-column), axis=1)
+
+
+def with_units(rows):
+    return jnp.concatenate([rows, jnp.ones((rows.shape[0], 3), rows.dtype)], axis=1)
+
+
+def attend_back(q, k_units, k, v_units, lse, grad, mix, usable):
+    scores = nt(k_units, extended(q, lse))
+    if usable is not None:
+        scores = jnp.where(usable, scores, MASKED)
+    probs = jnp.exp(scores)
+    inner = jnp.sum(grad.astype(SINGLE) * mix, axis=-1, keepdims=True)
+    grad_scores = (probs * nt(v_units, extended(grad, inner))).astype(NARROW)
+    return tn(grad_scores, k) * SCALE, mm(grad_scores, q), mm(probs.astype(NARROW), grad)
+
+
+def cross_back_kernel(carried_ref, gtime_ref, sec3_ref, sec2_ref, cq_ref, cmix_ref, clse_ref,
+                      kv_ref, usable_ref, text_ref, gains_ref, wtime_ref, wco_ref, wcq_ref,
+                      carried_out_ref, pack_ref, gain_ref,
+                      hat_s, back_s, dq_s, dkv_s, da_s, db_s, dw_s):
+    gain_ref[...] = jnp.zeros((8, C), SINGLE)
+    dkv_s[...] = jnp.zeros((TEXT, 2 * C), SINGLE)
+    usable = jnp.broadcast_to(usable_ref[...], (TEXT, STEP)) == 1
+    for r in range(STEPS):
+        rows = slice(r * STEP, (r + 1) * STEP)
+        part, gain, hat = ln_back_rows(sec3_ref[rows, :], gains_ref[4:5, :], nt(gtime_ref[rows, :], wtime_ref[...]))
+        gain_ref[1:2, :] += gain
+        hat_s[rows, :] = (hat * gains_ref[4:5, :]).astype(NARROW)
+        carried = carried_ref[rows, :] + part
+        back_s[rows, :] = carried.astype(NARROW)
+        gmix = nt(back_s[rows, :], wco_ref[...]).astype(NARROW)
+        for h in range(HEADS):
+            lanes = slice(h * HEAD, (h + 1) * HEAD)
+            lanes_v = slice(C + h * HEAD, C + (h + 1) * HEAD)
+            k = kv_ref[:, lanes]
+            dq, dk, dv = attend_back(
+                cq_ref[rows, lanes] * jnp.bfloat16(SCALE), with_units(k), k, with_units(kv_ref[:, lanes_v]),
+                clse_ref[rows, h : h + 1], gmix[:, lanes], cmix_ref[rows, lanes], usable,
+            )
+            dq_s[rows, lanes] = dq.astype(NARROW)
+            dkv_s[:, lanes] += dk
+            dkv_s[:, lanes_v] += dv
+        part, gain, hat = ln_back_rows(sec2_ref[rows, :], gains_ref[3:4, :], nt(dq_s[rows, :], wcq_ref[...]))
+        gain_ref[0:1, :] += gain
+        carried_out_ref[rows, :] = carried + part
+    da_s[...] = tn(hat_s[...], gtime_ref[...])
+    db_s[...] = tn(cmix_ref[...].astype(NARROW), back_s[...])
+    bands_out(pack_ref, 52, db_s, 20, 160)
+    for r in range(STEPS):
+        rows = slice(r * STEP, (r + 1) * STEP)
+        hat, rstd = ln_rows(sec2_ref[rows, :], None)
+        hat_s[rows, :] = (hat * gains_ref[3:4, :]).astype(NARROW)
+    db_s[...] = tn(hat_s[...], dq_s[...])
+    pair_out(pack_ref, 32, da_s, db_s)
+    dw_s[...] = tn(text_ref[...], dkv_s[...].astype(NARROW))
+    bands_out(pack_ref, 0, dw_s, 64, 320)
+
+
+def cross_back(*args):
+    low = ((PIX, C), NARROW)
+    return kernel_call(
+        cross_back_kernel,
+        [((PIX, C), SINGLE), (packed_shape(64), NARROW), ((8, C), SINGLE)],
+        [low, low, low, ((TEXT, 2 * C), SINGLE), ((C, 3 * C), SINGLE), ((C, C), SINGLE), ((CTX, 2 * C), SINGLE)],
+        flops=26 * 10**9,
+    )(*args)
+
+
+def self_back_kernel(carried_ref, sec1_ref, proj_ref, mix_ref, lse_ref, gains_ref, wqkv_ref, wso_ref,
+                     carried_out_ref, pack_ref, gain_ref,
+                     back_s, gmix_s, dproj_s, hat_s, dk_s, dv_s, da_s, db_s):
+    gain_ref[...] = jnp.zeros((8, C), SINGLE)
+    for r in range(STEPS):
+        rows = slice(r * STEP, (r + 1) * STEP)
+        back_s[rows, :] = carried_ref[rows, :].astype(NARROW)
+        gmix_s[rows, :] = nt(back_s[rows, :], wso_ref[...]).astype(NARROW)
+    db_s[...] = tn(mix_ref[...].astype(NARROW), back_s[...])
+    for h in range(HEADS):
+        lanes = slice(h * HEAD, (h + 1) * HEAD)
+        lanes_k = slice(C + h * HEAD, C + (h + 1) * HEAD)
+        lanes_v = slice(2 * C + h * HEAD, 2 * C + (h + 1) * HEAD)
+        k = proj_ref[:, lanes_k]
+        k_units = with_units(k)
+        v_units = with_units(proj_ref[:, lanes_v])
+        for r in range(STEPS):
+            rows = slice(r * STEP, (r + 1) * STEP)
+            dq, dk, dv = attend_back(
+                proj_ref[rows, lanes] * jnp.bfloat16(SCALE), k_units, k, v_units,
+                lse_ref[rows, h : h + 1], gmix_s[rows, lanes], mix_ref[rows, lanes], None,
+            )
+            dproj_s[rows, lanes] = dq.astype(NARROW)
+            if r == 0:
+                dk_s[...] = dk
+                dv_s[...] = dv
+            else:
+                dk_s[...] += dk
+                dv_s[...] += dv
+        dproj_s[:, lanes_k] = dk_s[...].astype(NARROW)
+        dproj_s[:, lanes_v] = dv_s[...].astype(NARROW)
+    for r in range(STEPS):
+        rows = slice(r * STEP, (r + 1) * STEP)
+        part, gain, hat = ln_back_rows(sec1_ref[rows, :], gains_ref[2:3, :], nt(dproj_s[rows, :], wqkv_ref[...]))
+        gain_ref[0:1, :] += gain
+        hat_s[rows, :] = (hat * gains_ref[2:3, :]).astype(NARROW)
+        carried_out_ref[rows, :] = carried_ref[rows, :] + part
+    da_s[...] = tn(hat_s[...], dproj_s[...])
+    pair_out(pack_ref, 0, da_s, db_s)
+
+
+def self_back_block(*args):
+    low = ((PIX, C), NARROW)
+    return kernel_call(
+        self_back_kernel,
+        [((PIX, C), SINGLE), (packed_shape(24), NARROW), ((8, C), SINGLE)],
+        [low, low, ((PIX, 3 * C), NARROW), low, ((PIX, HEAD), SINGLE), ((PIX, HEAD), SINGLE),
+         ((C, 3 * C), SINGLE), ((C, C), SINGLE)],
+        flops=29 * 10**9,
+    )(*args)
+
+
+def feed_kernel(sec3_ref, mix_ref, cot_ref, gains_ref, wto_ref, wup_ref, wdown_ref,
+                out_ref, carried_ref, gmix_ref, pack_ref, gain_ref,
+                hat_s, act_s, lift_s, back_s, d_s, dw_s):
+    gain_ref[...] = jnp.zeros((8, C), SINGLE)
+    for r in range(STEPS):
+        rows = slice(r * STEP, (r + 1) * STEP)
+        sec4 = sec3_ref[rows, :] + mm(mix_ref[rows, :], wto_ref[...])
+        hat, rstd = ln_rows(sec4, None)
+        hat_s[rows, :] = (hat * gains_ref[5:6, :]).astype(NARROW)
+        lifted = mm(hat_s[rows, :], wup_ref[...])
+        cube = lifted * lifted
+        inner = jnp.tanh(GELU_A * lifted * (1.0 + GELU_B * cube))
+        gate = 0.5 + 0.5 * inner
+        act_s[rows, :] = (lifted * gate).astype(NARROW)
+        slope = gate + (0.5 * GELU_A) * lifted * (1.0 - inner * inner) * (1.0 + (3.0 * GELU_B) * cube)
+        grad_act = nt(cot_ref[rows, :], wdown_ref[...])
+        lift_s[rows, :] = (grad_act * slope).astype(NARROW)
+        out_ref[rows, :] = (sec4 + mm(act_s[rows, :], wdown_ref[...])).astype(NARROW)
+        part, gain, hat = ln_back_rows(sec4, gains_ref[5:6, :], nt(lift_s[rows, :], wup_ref[...]))
+        gain_ref[0:1, :] += gain
+        carried = cot_ref[rows, :].astype(SINGLE) + part
+        carried_ref[rows, :] = carried
+        back_s[rows, :] = carried.astype(NARROW)
+        gmix_ref[rows, :] = nt(back_s[rows, :], wto_ref[...]).astype(NARROW)
+    dw_s[...] = tn(hat_s[...], lift_s[...])
+    bands_out(pack_ref, 0, dw_s, 20, 640)
+    d_s[...] = tn(act_s[...], cot_ref[...])
+    bands_out(pack_ref, 20, d_s, 80, 160)
+    d_s[0:C, :] = tn(mix_ref[...], back_s[...])
+    bands_out(pack_ref, 40, d_s, 20, 160)
+
+
+def feed_block(*args):
+    low = ((PIX, C), NARROW)
+    wide = ((PIX, FF), NARROW)
+    return kernel_call(
+        feed_kernel,
+        [low, ((PIX, C), SINGLE), low, (packed_shape(48), NARROW), ((8, C), SINGLE)],
+        [low, wide, wide, low, ((FF, C), SINGLE), ((C, FF), SINGLE)],
+        flops=20 * 10**9,
+    )(*args)
+
+
+def untile(tile):
+    return tile.reshape(16, 8, tile.shape[-1])
+
+
+def time_kernel(qkv_ref, bias_ref, low_ref, mix_ref, lse_ref, wide_s):
+    wide_s[...] = qkv_ref[...].astype(SINGLE)
+    for b in range(PIX // 16 // 8):
+        tile = wide_s[:, 8 * b : 8 * b + 8, :].reshape(128, 3 * C).astype(NARROW)
+        mixes = []
+        for h in range(HEADS):
+            q = tile[:, h * HEAD : (h + 1) * HEAD] * jnp.bfloat16(SCALE)
+            k = tile[:, C + h * HEAD : C + (h + 1) * HEAD]
+            v = with_ones(tile[:, 2 * C + h * HEAD : 2 * C + (h + 1) * HEAD])
+            scores = nt(q, k) + bias_ref[h]
+            highest = jnp.max(scores, axis=-1, keepdims=True)
+            both = mm(jnp.exp(scores - highest).astype(NARROW), v)
+            total = both[:, HEAD : HEAD + 1]
+            mixes.append(both[:, :HEAD] / total)
+            lse_ref[128 * b : 128 * b + 128, h : h + 1] = highest + jnp.log(total)
+        mix_ref[:, 8 * b : 8 * b + 8, :] = untile(jnp.concatenate(mixes, axis=1))
+    low_ref[...] = mix_ref[...].astype(NARROW)
+
+
+def time_block(qkv, bias):
+    rows = PIX // 16
+    return kernel_call(
+        time_kernel,
+        [((16, rows, C), NARROW), ((16, rows, C), SINGLE), ((PIX, 8), SINGLE)],
+        [((16, rows, 3 * C), SINGLE)],
+        flops=15 * 10**9,
+    )(qkv, bias)
+
+
+def time_back_kernel(qkv_ref, bias_ref, mix_ref, lse_ref, grad_ref, dqkv_ref, dbias_ref, wide_s, grad_s, out_s):
+    dbias_ref[...] = jnp.zeros((HEADS, 128, 128), SINGLE)
+    wide_s[...] = qkv_ref[...].astype(SINGLE)
+    grad_s[...] = grad_ref[...].astype(SINGLE)
+    for b in range(PIX // 16 // 8):
+        part = slice(8 * b, 8 * b + 8)
+        tile = wide_s[:, part, :].reshape(128, 3 * C).astype(NARROW)
+        grads = grad_s[:, part, :].reshape(128, C)
+        inners = grads * mix_ref[:, part, :].reshape(128, C)
+        grads = grads.astype(NARROW)
+        dqs, dks, dvs = [], [], []
+        for h in range(HEADS):
+            lanes = slice(h * HEAD, (h + 1) * HEAD)
+            q = tile[:, lanes] * jnp.bfloat16(SCALE)
+            k = tile[:, C + h * HEAD : C + (h + 1) * HEAD]
+            v = tile[:, 2 * C + h * HEAD : 2 * C + (h + 1) * HEAD]
+            g = grads[:, lanes]
+            lse = lse_ref[128 * b : 128 * b + 128, h : h + 1]
+            probs = jnp.exp(nt(with_units(k), extended(q, lse)) + bias_ref[h])
+            inner = jnp.sum(inners[:, lanes], axis=-1, keepdims=True)
+            ds = (probs * nt(with_units(v), extended(g, inner))).astype(NARROW)
+            dbias_ref[h] += ds.astype(SINGLE)
+            dqs.append(tn(ds, k) * SCALE)
+            dks.append(mm(ds, q))
+            dvs.append(mm(probs.astype(NARROW), g))
+        out_s[:, part, :] = untile(jnp.concatenate(dqs + dks + dvs, axis=1))
+    dqkv_ref[...] = out_s[...].astype(NARROW)
+
+
+def time_back_block(qkv, bias_t, mix, lse, grad):
+    wide = ((16, PIX // 16, 3 * C), SINGLE)
+    return kernel_call(
+        time_back_kernel,
+        [((16, PIX // 16, 3 * C), NARROW), ((HEADS, 128, 128), SINGLE)],
+        [wide, ((16, PIX // 16, C), SINGLE), wide],
+        flops=25 * 10**9,
+    )(qkv, bias_t, mix, lse, grad)
+
+
+def conv_back_rows(y_s, r):
+    not_first, not_last = edge_masks(STEP)
+    base = r * STEP
+    sides = []
+    for j in range(3):
+        total = None
+        for i in range(3):
+            lanes = slice((3 * i + j) * C, (3 * i + j + 1) * C)
+            part = y_s[pl.ds(base + IMG_W * (2 - i), STEP), lanes]
+            total = part if total is None else total + part
+        sides.append(total)
+    from_next = jnp.where(not_last, pltpu.roll(sides[0], STEP - 1, 0), 0.0)
+    from_prev = jnp.where(not_first, pltpu.roll(sides[2], 1, 0), 0.0)
+    return from_next + sides[1] + from_prev
+
+
+def conv_weight_grad(cols_ref, back_s, d_s):
+    for i in range(3):
+        d_s[3 * C * i : 3 * C * (i + 1), :] = tn(cols_ref[pl.ds(IMG_W * i, PIX), :], back_s[...])
+
+
+def conv_input_products(back_s, w_ref, y_s):
+    border = jnp.zeros((IMG_W, 9 * C), SINGLE)
+    y_s[0:IMG_W, :] = border
+    y_s[PIX + IMG_W :, :] = border
+    for r in range(STEPS):
+        y_s[pl.ds(IMG_W + r * STEP, STEP), :] = nt(back_s[r * STEP : (r + 1) * STEP, :], w_ref[...])
+
+
+def silu_slope(pre):
+    gate = 0.5 + 0.5 * jnp.tanh(0.5 * pre)
+    return gate * (1.0 + pre * (1.0 - gate))
+
+
+def second_weight_kernel(carried_ref, cols2_ref, upper_ref, pack_ref, back_ref, d_s):
+    pack_ref[:, :, :, 0:24, :] = upper_ref[...]
+    for r in range(STEPS):
+        rows = slice(r * STEP, (r + 1) * STEP)
+        back_ref[rows, :] = carried_ref[rows, :].astype(NARROW)
+    conv_weight_grad(cols2_ref, back_ref, d_s)
+    bands_out(pack_ref, 24, d_s, 180, 160)
+
+
+def second_weight(carried, cols2, upper):
+    return kernel_call(
+        second_weight_kernel, [(packed_shape(72), NARROW), ((PIX, C), NARROW)], [((9 * C, C), SINGLE)],
+        flops=9 * 10**9,
+    )(carried, cols2, upper)
+
+
+def second_back_kernel(back_s, conv_out_ref, stats_ref, film_ref, gains_ref, gmat_ref,
+                       w2_ref, hidden_ref, back_ref, sums_ref, y_s):
+    conv_input_products(back_s, w2_ref, y_s)
+    scale = 1.0 + film_ref[0:1, :C]
+    shift = film_ref[0:1, C:]
+    center, spread, gain = stats_ref[2:3, :], stats_ref[3:4, :], gains_ref[1:2, :]
+    zero = jnp.zeros((1, C), SINGLE)
+    gain_sum, total, crossed = zero, zero, zero
+    for r in range(STEPS):
+        rows = slice(r * STEP, (r + 1) * STEP)
+        normed = (conv_out_ref[rows, :] * scale + shift - center) * spread
+        grad_pre = conv_back_rows(y_s, r) * silu_slope(normed * gain)
+        gain_sum += jnp.sum(grad_pre * normed, axis=0, keepdims=True)
+        grad = grad_pre * gain
+        hidden_ref[rows, :] = grad
+        total += jnp.sum(grad, axis=0, keepdims=True)
+        crossed += jnp.sum(grad * normed, axis=0, keepdims=True)
+    members = PIX * (C // GROUPS)
+    total = grouped(total, gmat_ref[...]) / members
+    crossed = grouped(crossed, gmat_ref[...]) / members
+    film_one, film_two = zero, zero
+    for r in range(STEPS):
+        rows = slice(r * STEP, (r + 1) * STEP)
+        conv_out = conv_out_ref[rows, :]
+        normed = (conv_out * scale + shift - center) * spread
+        hidden = spread * (hidden_ref[rows, :] - total - normed * crossed)
+        film_one += jnp.sum(hidden * conv_out, axis=0, keepdims=True)
+        film_two += jnp.sum(hidden, axis=0, keepdims=True)
+        back_ref[rows, :] = (hidden * scale).astype(NARROW)
+    sums_ref[...] = jnp.zeros((8, C), SINGLE)
+    sums_ref[0:1, :] = gain_sum
+    sums_ref[1:2, :] = film_one
+    sums_ref[2:3, :] = film_two
+
+
+def second_back(*args):
+    return kernel_call(
+        second_back_kernel,
+        [((PIX, C), SINGLE), ((PIX, C), NARROW), ((8, C), SINGLE)],
+        [((PIX + 2 * IMG_W, 9 * C), SINGLE)],
+        flops=9 * 10**9,
+    )(*args)
+
+
+def first_weight_kernel(cols1_ref, back_ref, pack_ref, d_s):
+    conv_weight_grad(cols1_ref, back_ref, d_s)
+    bands_out(pack_ref, 0, d_s, 180, 160)
+
+
+def first_weight(cols1, back):
+    return kernel_call(
+        first_weight_kernel, [(packed_shape(48), NARROW)], [((9 * C, C), SINGLE)], flops=9 * 10**9
+    )(cols1, back)[0]
+
+
+def small_kernel(half_ref, got_ref, own_ref, other_ref, small_ref):
+    half = half_ref[0]
+
+    def film(place):
+        both = got_ref[:, place, :]
+        return lax.dot_general(
+            both[:, C : C + 80], both[:, :C], TN, precision=PRECISE, preferred_element_type=SINGLE
+        )
+
+    own_ref[...] = film(half)
+    other_ref[...] = film(1 - half).astype(NARROW)
+    total = got_ref[0]
+    for s in range(1, 16):
+        total += got_ref[s]
+    small_ref[...] = total
+
+
+def small_settle(temb, sums_d, sums_e, gain_a, gain_b, gain_c, grad_table, half_vec):
+    grad_film = jnp.concatenate([sums_d[1:2], sums_d[2:3]]).reshape(1, 1, 2, 1, C)
+    cut = temb[0].astype(SINGLE).reshape(2, 8, 1, 1, 80).transpose(1, 2, 0, 3, 4)
+    factors = jnp.concatenate(
+        [jnp.broadcast_to(grad_film.transpose(0, 2, 1, 3, 4), (8, 2, 2, 1, C)),
+         jnp.broadcast_to(cut, (8, 2, 2, 1, 80)), jnp.zeros((8, 2, 2, 1, BAND - C - 80), SINGLE)],
+        axis=-1,
+    ).reshape(16, 2, BAND)
+    table_row = jnp.pad(grad_table.reshape(1, -1), ((0, 0), (0, C - NB * HEADS)))
+    rows = jnp.concatenate([sums_e[0:1], sums_d[0:1], gain_c[0:1], gain_b[0:2], gain_a[0:1], table_row])
+    rows = jnp.broadcast_to(jnp.pad(rows, ((0, 0), (0, BAND - C))), (16, 7, BAND))
+    pad = jnp.zeros((16, 7, BAND), SINGLE)
+    got = lax.all_to_all(jnp.concatenate([factors, rows, pad], axis=1), CUBE, 0, 0, tiled=True)
+    own, other, small = smem_call(
+        small_kernel, 1, [((80, C), SINGLE), ((80, C), NARROW), ((16, BAND), SINGLE)], flops=2 * 10**9
+    )(half_vec, got)
+    swap = [(0, 1), (1, 0)]
+    return own, lax.ppermute(other, HALF, swap), small + lax.ppermute(small, HALF, swap)
+
+
+def finish_kernel(down, down_r, middle, middle_r, upper, upper_r, first, first_r,
+                  film, film_r, *outs):
+    w = Weights(*outs)
+    total = down[...] + down_r[...].astype(SINGLE)
+    bands_in(total, 0, w.feed_up, 20, 640)
+    bands_in(total, 20, w.feed_down, 80, 160)
+    bands_in(total, 40, w.time_output, 20, 160)
+    total = middle[...] + middle_r[...].astype(SINGLE)
+    bands_in(total, 0, w.cross_keyval, 64, 320)
+    w.time_project[...] = total[32:52, 0:480]
+    w.cross_query[...] = total[32:52, 480:640]
+    bands_in(total, 52, w.cross_output, 20, 160)
+    total = upper[...] + upper_r[...].astype(SINGLE)
+    w.self_project[...] = total[0:20, 0:480]
+    w.self_output[...] = total[0:20, 480:640]
+    bands_in(total, 24, w.conv_second, 180, 160)
+    bands_in(first[...] + first_r[...].astype(SINGLE), 0, w.conv_first, 180, 160)
+    w.film_weight[...] = film[...] + film_r[...].astype(SINGLE)
+
+
+def finish(*groups):
+    shapes = Weights(
+        conv_first=(180, 160), conv_second=(180, 160), film_weight=(80, C), self_project=(20, 480),
+        self_output=(20, 160), cross_query=(20, 160), cross_keyval=(64, C), cross_output=(20, 160),
+        time_project=(20, 480), time_output=(20, 160), feed_up=(20, BAND), feed_down=(80, 160),
+    )
+    return Weights(*kernel_call(finish_kernel, [(s, SINGLE) for s in shapes])(*groups))
+
+
+def first_back_kernel(carried_ref, x_ref, stats_ref, gains_ref, gmat_ref, w1_ref, back_ref,
+                      grad_ref, sums_ref, y_s, pre_s):
+    conv_input_products(back_ref, w1_ref, y_s)
+    center, spread, gain = stats_ref[0:1, :], stats_ref[1:2, :], gains_ref[0:1, :]
+    zero = jnp.zeros((1, C), SINGLE)
+    gain_sum, total, crossed = zero, zero, zero
+    for r in range(STEPS):
+        rows = slice(r * STEP, (r + 1) * STEP)
+        normed = (x_ref[rows, :].astype(SINGLE) - center) * spread
+        grad_pre = conv_back_rows(y_s, r) * silu_slope(normed * gain)
+        gain_sum += jnp.sum(grad_pre * normed, axis=0, keepdims=True)
+        grad = grad_pre * gain
+        pre_s[rows, :] = grad
+        total += jnp.sum(grad, axis=0, keepdims=True)
+        crossed += jnp.sum(grad * normed, axis=0, keepdims=True)
+    members = PIX * (C // GROUPS)
+    total = grouped(total, gmat_ref[...]) / members
+    crossed = grouped(crossed, gmat_ref[...]) / members
+    for r in range(STEPS):
+        rows = slice(r * STEP, (r + 1) * STEP)
+        normed = (x_ref[rows, :].astype(SINGLE) - center) * spread
+        grad = spread * (pre_s[rows, :] - total - normed * crossed)
+        grad_ref[rows, :] = (carried_ref[rows, :] + grad).astype(NARROW)
+    sums_ref[...] = jnp.zeros((8, C), SINGLE)
+    sums_ref[0:1, :] = gain_sum
+
+
+def first_back(*args):
+    return kernel_call(
+        first_back_kernel,
+        [((PIX, C), NARROW), ((8, C), SINGLE)],
+        [((PIX + 2 * IMG_W, 9 * C), SINGLE), ((PIX, C), SINGLE)],
+        flops=11 * 10**9,
+    )(*args)
+
+
+BAND = 640
+QUARTER = 160
+PACK_ROWS = 272
+
+
+def smem_call(body, n_in, outs, scratch=(), flops=10**9):
+    specs = [pl.BlockSpec(memory_space=pltpu.SMEM)] + [pl.BlockSpec(memory_space=pltpu.VMEM)] * n_in
+    return pl.pallas_call(
+        body,
+        in_specs=specs,
+        out_shape=[jax.ShapeDtypeStruct(s, d) for s, d in outs],
+        scratch_shapes=[pltpu.VMEM(s, d) for s, d in scratch],
+        compiler_params=pltpu.CompilerParams(vmem_limit_bytes=VMEM_BYTES),
+        cost_estimate=pl.CostEstimate(flops=flops, bytes_accessed=10**7, transcendentals=0),
+    )
+
+
+def side_by_side(out, at, ref, cols):
+    parts = BAND // cols
+    tall = ref.shape[0] // parts
+    wide = ref[...].astype(SINGLE)
+    out[at : at + tall, :] = jnp.concatenate(
+        [wide[tall * q : tall * (q + 1), :] for q in range(parts)], axis=1
+    ).astype(NARROW)
+
+
+def pack_kernel(*refs):
+    w = Weights(*refs[:12])
+    out = refs[12]
+    out[...] = jnp.zeros((PACK_ROWS, BAND), NARROW)
+    side_by_side(out, 0, w.conv_first, 160)
+    side_by_side(out, 48, w.conv_second, 160)
+    side_by_side(out, 96, w.film_weight, 320)
+    side_by_side(out, 136, w.cross_keyval, 320)
+    out[168:188, 0:480] = w.self_project[...]
+    out[168:188, 480:640] = w.self_output[...]
+    out[192:212, 0:480] = w.time_project[...]
+    out[192:212, 480:640] = w.time_output[...]
+    out[216:236, :] = w.feed_up[...]
+    side_by_side(out, 240, w.feed_down, 160)
+    side_by_side(out, 260, w.cross_query, 160)
+    side_by_side(out, 265, w.cross_output, 160)
+
+
+def pack_weights(w):
+    return kernel_call(pack_kernel, [((PACK_ROWS, BAND), NARROW)])(*w)[0]
+
+
+def unpack_kernel(half_ref, full_ref, *outs):
+    w = Weights(*outs)
+    half = half_ref[0]
+    unpack_tall(half, full_ref, w.conv_first, 0, 180, 160)
+    unpack_tall(half, full_ref, w.conv_second, 48, 180, 160)
+    unpack_tall(half, full_ref, w.film_weight, 96, 80, 320)
+    unpack_tall(half, full_ref, w.cross_keyval, 136, 64, 320)
+    unpack_tall(half, full_ref, w.feed_up, 216, 20, 640)
+    unpack_tall(half, full_ref, w.feed_down, 240, 80, 160)
+    unpack_tall(half, full_ref, w.cross_query, 260, 20, 160)
+    unpack_tall(half, full_ref, w.cross_output, 265, 20, 160)
+    for out, at, c0, cols in (
+        (w.self_project, 168, 0, 480), (w.self_output, 168, 480, 160),
+        (w.time_project, 192, 0, 480), (w.time_output, 192, 480, 160),
+    ):
+        for quad in range(4):
+            parts = []
+            for f in range(4 * quad, 4 * quad + 4):
+                place = half if f < 8 else 1 - half
+                parts.append(jnp.concatenate(
+                    [full_ref[2 * (f % 8) + s, place, at : at + 20, c0 : c0 + cols].astype(SINGLE) for s in range(2)],
+                    axis=1,
+                ))
+            out[80 * quad : 80 * (quad + 1), :] = jnp.concatenate(parts, axis=0).astype(NARROW)
+
+
+def unpack_weights(half_vec, full):
+    shapes = [
+        (9 * C, C), (9 * C, C), (TEMB, 2 * C), (C, 3 * C), (C, C), (C, C), (CTX, 2 * C), (C, C), (C, 3 * C),
+        (C, C), (C, FF), (FF, C),
+    ]
+    out = smem_call(unpack_kernel, 1, [(s, NARROW) for s in shapes], flops=10 * 10**9)(half_vec, full)
+    return Weights(*out)
+
+
+def packed_shape(rows):
+    return (2, 8, 2, rows, BAND)
+
+
+def bands_out(out_ref, at, grad_ref, rows, cols):
+    parts = BAND // cols
+    tall = rows // parts
+    for f in range(16):
+        for s in range(2):
+            lanes = slice(s * cols, (s + 1) * cols)
+            pieces = [
+                grad_ref[rows * f + tall * q : rows * f + tall * (q + 1), lanes] for q in range(parts)
+            ]
+            piece = pieces[0] if parts == 1 else jnp.concatenate(pieces, axis=1)
+            out_ref[f % 2, 2 * (f % 8 // 2) + s, f // 8, at : at + tall, :] = piece.astype(NARROW)
+
+
+def pair_out(out_ref, at, wide_ref, thin_ref):
+    for f in range(16):
+        for s in range(2):
+            piece = jnp.concatenate(
+                [wide_ref[20 * f : 20 * f + 20, 480 * s : 480 * s + 480],
+                 thin_ref[20 * f : 20 * f + 20, 160 * s : 160 * s + 160]],
+                axis=1,
+            )
+            out_ref[f % 2, 2 * (f % 8 // 2) + s, f // 8, at : at + 20, :] = piece.astype(NARROW)
+
+
+def bands_in(total, at, out_ref, rows, cols):
+    parts = BAND // cols
+    tall = rows // parts
+    for q in range(parts):
+        out_ref[tall * q : tall * (q + 1), :] = total[at : at + tall, cols * q : cols * (q + 1)]
+
+
+def reduce_kernel(half_ref, got_ref, own_ref, other_ref):
+    half = half_ref[0]
+    own = got_ref[0, half].astype(SINGLE)
+    other = got_ref[0, 1 - half].astype(SINGLE)
+    for s in range(1, 8):
+        own += got_ref[s, half].astype(SINGLE)
+        other += got_ref[s, 1 - half].astype(SINGLE)
+    own_ref[...] = own
+    other_ref[...] = other.astype(NARROW)
+
+
+def chip_sum(packed, core):
+    got = lax.ppermute(pick(1 - core, packed), CORE, [(0, 1), (1, 0)])
+    return (pick(core, packed).astype(SINGLE) + got.astype(SINGLE)).astype(NARROW)
+
+
+def chip_swap(chip):
+    return lax.all_to_all(chip, CHIPS, 0, 0, tiled=True)
+
+
+def reduce_half(got, half_vec):
+    shape = got.shape[2:]
+    own, other = smem_call(reduce_kernel, 1, [(shape, SINGLE), (shape, NARROW)], flops=2 * 10**9)(half_vec, got)
+    return own, lax.ppermute(other, HALF, [(0, 1), (1, 0)])
+
+
+def time_setup(video_mask, video_number, bucket_index, bias_table, half):
+    order = jnp.array([8 * (g % 2) + g // 2 for g in range(16)])
+    live = pick(half, video_mask)
+    number = pick(half, video_number)
+    same = (live[:, None] == 1) & (live[None, :] == 1) & (number[:, None] == number[None, :])
+    same = same | (jnp.arange(16)[:, None] == jnp.arange(16)[None, :])
+    bucket = bucket_index[order][:, order]
+    one_hot = (bucket.reshape(-1, 1) == jnp.arange(NB)[None, :]).astype(SINGLE)
+    table = jnp.dot(one_hot, bias_table, precision=PRECISE).reshape(16, 16, HEADS).transpose(2, 0, 1)
+    small = jnp.where(same[order][:, order][None], table, MASKED)
+    pixel = jnp.arange(8)
+    wide = jnp.where(
+        (pixel[:, None] == pixel[None, :])[None, None, :, None, :], small[:, :, None, :, None], MASKED
+    )
+    return wide.reshape(HEADS, 128, 128), one_hot
+
+
+def swap_frames(block, rows):
+    return lax.all_to_all(block.reshape(16, rows, block.shape[-1]), CUBE, 0, 0, tiled=True)
+
+
+def fast_shards(
+    video_in, time_embed, text_embed, text_mask, video_mask, video_number, bucket_index,
+    norm_gains, bias_table, conv_first, conv_second, film_weight, self_project, self_output,
+    cross_query, cross_keyval, cross_output, time_project, time_output, feed_up, feed_down,
+    cotangent,
+):
+    half = lax.axis_index(HALF)
+    space = lax.axis_index(SPACE)
+    core = lax.axis_index(CORE)
+    gains = norm_gains.T
+    half_vec = jnp.full((1,), half, jnp.int32)
+    packed = pack_weights(Weights(
+        conv_first=conv_first, conv_second=conv_second, film_weight=film_weight,
+        self_project=self_project, self_output=self_output, cross_query=cross_query,
+        cross_keyval=cross_keyval, cross_output=cross_output, time_project=time_project,
+        time_output=time_output, feed_up=feed_up, feed_down=feed_down,
+    ))
+    other = lax.ppermute(packed, HALF, [(0, 1), (1, 0)])
+    full = lax.all_gather(jnp.stack([packed, other]), CUBE, axis=0, tiled=False)
+    video_in, other = lax.optimization_barrier((video_in, other))
+    x = to_slot(video_in.reshape(FR_DEV, -1, C), half, space)
+    text_embed, cotangent, full = lax.optimization_barrier((text_embed, cotangent, full))
+    w = unpack_weights(half_vec, full)
+    cot = to_slot(cotangent.reshape(FR_DEV, -1, C), half, space)
+    text = to_slot(text_embed.reshape(FR_DEV, -1, CTX), half, space)
+    temb = meta_slot(time_embed.reshape(FR_DEV, 1, TEMB), space)
+    usable = meta_slot(text_mask.reshape(FR_DEV, 1, TEXT), space)[0] == 1
+    temb_act = jax.nn.silu(temb.astype(SINGLE)).astype(NARROW)
+    bias, one_hot = time_setup(video_mask, video_number, bucket_index, bias_table, half)
+    gmat = group_matrix()
+
+    temb_act = jnp.broadcast_to(temb_act, (8, TEMB))
+    conv_out, sec1, cols1, cols2, stats, film = conv_block(
+        x, w.conv_first, w.conv_second, temb_act, w.film_weight, gains, gmat
+    )
+    proj, mix, lse, sec2, text_kv, cq, cmix, clse, sec3, time_proj = attn_block(
+        sec1, gains, w.self_project, w.self_output, text, usable[None, :], w.cross_keyval,
+        w.cross_query, w.cross_output, w.time_project,
+    )
+    time_qkv = swap_frames(time_proj, PIX // 16)
+    time_low, time_mix_t, time_lse = time_block(time_qkv, bias)
+    time_mix = swap_frames(time_low, PIX // 16).reshape(PIX, C)
+    result, carried, grad_time_mix, packed, gain_a = feed_block(
+        sec3, time_mix, cot, gains, w.time_output, w.feed_up, w.feed_down
+    )
+    grad_mix_t = swap_frames(grad_time_mix, PIX // 16)
+    packed, result, grad_mix_t = lax.optimization_barrier((packed, result, grad_mix_t))
+    chip_down = chip_sum(packed, core)
+    chip_down, grad_mix_t = lax.optimization_barrier((chip_down, grad_mix_t))
+    down = chip_swap(chip_down)
+    grad_qkv_t, bias_grad = time_back_block(time_qkv, bias.transpose(0, 2, 1), time_mix_t, time_lse, grad_mix_t)
+    grad_qkv_t, down = lax.optimization_barrier((grad_qkv_t, down))
+    grad_time_proj = swap_frames(grad_qkv_t, PIX // 16).reshape(PIX, 3 * C)
+    grad_time_proj, result, down = lax.optimization_barrier((grad_time_proj, result, down))
+    block_out = from_slot(result, half, space).reshape(video_in.shape)
+    small = jnp.sum(bias_grad.reshape(HEADS, 16, 8, 16, 8), axis=(2, 4)).transpose(2, 1, 0)
+    grad_table = jnp.dot(one_hot.T, small.reshape(-1, HEADS), precision=PRECISE)
+    carried, packed, gain_b = cross_back(
+        carried, grad_time_proj, sec3, sec2, cq, cmix, clse, text_kv, usable[:, None], text, gains,
+        w.time_project, w.cross_output, w.cross_query,
+    )
+    carried, packed, block_out, down, grad_table = lax.optimization_barrier(
+        (carried, packed, block_out, down, grad_table)
+    )
+    down = reduce_half(down, half_vec)
+    chip_middle = chip_sum(packed, core)
+    carried, chip_middle = lax.optimization_barrier((carried, chip_middle))
+    middle = chip_swap(chip_middle)
+    carried, packed, gain_c = self_back_block(
+        carried, sec1, proj, mix, lse, gains, w.self_project, w.self_output
+    )
+    packed, back_second = second_weight(carried, cols2, packed)
+    back_second, middle, packed = lax.optimization_barrier((back_second, middle, packed))
+    middle = reduce_half(middle, half_vec)
+    chip_upper = chip_sum(packed, core)
+    _, back_first, sums_d = second_back(
+        back_second, conv_out, stats, film, gains, gmat, w.conv_second
+    )
+    back_first, chip_upper, sums_d = lax.optimization_barrier((back_first, chip_upper, sums_d))
+    upper = chip_swap(chip_upper)
+    packed = first_weight(cols1, back_first)
+    chip_first = chip_sum(packed, core)
+    back_first, chip_first = lax.optimization_barrier((back_first, chip_first))
+    first = chip_swap(chip_first)
+    grad_x, sums_e = first_back(carried, x, stats, gains, gmat, w.conv_first, back_first)
+    input_grad = from_slot(grad_x, half, space).reshape(video_in.shape)
+    film_own, film_got, small = small_settle(
+        temb_act, sums_d, sums_e, gain_a, gain_b, gain_c, grad_table, half_vec
+    )
+    upper = reduce_half(upper, half_vec)
+    first = reduce_half(first, half_vec)
+    gain_sum = small[2:8, :C].T
+    out = finish(*down, *middle, *upper, *first, film_own, film_got)
+    return (
+        block_out, input_grad, gain_sum, small[8, : NB * HEADS].reshape(NB, HEADS),
+        out.conv_first, out.conv_second, out.film_weight, out.self_project, out.self_output,
+        out.cross_query, out.cross_keyval, out.cross_output, out.time_project, out.time_output,
+        out.feed_up, out.feed_down,
+    )
+
+
+def fast_solution(mesh):
+    split = Mesh(mesh.devices.reshape(2, 4, 2, 2), WORLD)
+    frames = (HALF, QUAD, CORE)
+    image = P(None, frames, SPACE, None, None)
+    weight = P(frames, SPACE)
+    placed = (
+        image, P(None, frames, None), P(None, frames, SPACE, None), P(None, frames, None),
+        P(), P(), P(), P(), P(),
+    ) + (weight,) * 12 + (image,)
+    return jax.shard_map(
+        fast_shards, mesh=split, in_specs=placed,
+        out_specs=(image, image, P(), P()) + (weight,) * 12, check_vma=False,
+    )
+
+
 def solution(mesh):
+    if mesh.shape[FRAME] == GROUP_LEN and mesh.shape[SPACE] == FR_DEV:
+        return fast_solution(mesh)
     placed = (
-        P(None, "frame", "space", None, None),
-        P(None, "frame", None),
-        P(None, "frame", "space", None),
-        P(None, "frame", None),
+        P(None, FRAME, SPACE, None, None),
+        P(None, FRAME, None),
+        P(None, FRAME, SPACE, None),
+        P(None, FRAME, None),
         P(),
         P(),
         P(),
         P(),
         P(),
-        P("frame", "space"),
-        P("frame", "space"),
-        P("frame", "space"),
-        P("frame", "space"),
-        P("frame", "space"),
-        P("frame", "space"),
-        P("frame", "space"),
-        P("frame", "space"),
-        P("frame", "space"),
-        P("frame", "space"),
-        P("frame", "space"),
-        P("frame", "space"),
-        P(None, "frame", "space", None, None),
+        P(FRAME, SPACE),
+        P(FRAME, SPACE),
+        P(FRAME, SPACE),
+        P(FRAME, SPACE),
+        P(FRAME, SPACE),
+        P(FRAME, SPACE),
+        P(FRAME, SPACE),
+        P(FRAME, SPACE),
+        P(FRAME, SPACE),
+        P(FRAME, SPACE),
+        P(FRAME, SPACE),
+        P(FRAME, SPACE),
+        P(None, FRAME, SPACE, None, None),
     )
     return jax.shard_map(
         shards,
         mesh=mesh,
         in_specs=placed,
         out_specs=(
-            P(None, "frame", "space", None, None),
-            P(None, "frame", "space", None, None),
+            P(None, FRAME, SPACE, None, None),
+            P(None, FRAME, SPACE, None, None),
             P(),
             P(),
-            P("frame", "space"),
-            P("frame", "space"),
-            P("frame", "space"),
-            P("frame", "space"),
-            P("frame", "space"),
-            P("frame", "space"),
-            P("frame", "space"),
-            P("frame", "space"),
-            P("frame", "space"),
-            P("frame", "space"),
-            P("frame", "space"),
-            P("frame", "space"),
+            P(FRAME, SPACE),
+            P(FRAME, SPACE),
+            P(FRAME, SPACE),
+            P(FRAME, SPACE),
+            P(FRAME, SPACE),
+            P(FRAME, SPACE),
+            P(FRAME, SPACE),
+            P(FRAME, SPACE),
+            P(FRAME, SPACE),
+            P(FRAME, SPACE),
+            P(FRAME, SPACE),
+            P(FRAME, SPACE),
         ),
         check_vma=False,
     )

time: 2250 us -> 646 us (0.29)
  waiting for transfers between devices: 973 us -> 206 us
  local copies, waits for them, and re-layouts: 451 us -> 36.4 us
  blocking collectives: 441 us -> 40.4 us
  Pallas kernels: 0 us -> 218 us
  matrix products: 161 us -> 0.42 us
  other arithmetic: 155 us -> 27.7 us
  starting transfers between devices: 30.7 us -> 89.1 us
    all_gather x12 -> x1, waiting for transfers between devices: 456 us -> 63.2 us  [fast_shards(): full = lax.all_gather(jnp.stack([packed, other]), CUBE, axis=0, tiled=False)]
    all_gather x22 -> x0, blocking collectives: 339 us -> none  [the longest x4 89.1 us: collect(): lax.all_gather(item_one, 'frame', axis=0, tiled=True)]
    reduce_scatter x13 -> x0, waiting for transfers between devices: 285 us -> none  [the longest x2 263 us: return_keys(): lax.psum_scatter(spread_grads.astype(jnp.bfloat16), 'frame', scatter_dime...]
    pallas_call x0 -> x19, Pallas kernels: none -> 218 us  [the longest x1 28.4 us: self_back_block(): kernel_call(self_back_kernel, [((PIX, C), SINGLE), (packed_shape(24), NAR...]
    unnamed x33 -> x1, waiting for transfers between devices: 188 us -> 0.02 us
    dot_general x56 -> x2, matrix products: 161 us -> 0.42 us  [the longest x1 0.22 us: fast_shards(): grad_table = jnp.dot(one_hot.T, small.reshape(-1, HEADS), precision=PRECISE)]
    while x48 -> x0, local copies, waits for them, and re-layouts: 95.2 us -> none
    ppermute x8 -> x23, waiting for transfers between devices: 5.23 us -> 90.1 us  [the longest x2 49.9 us: from_slot(): lax.ppermute(pick(1 - half, pieces), PAIR, [(d, s) for s, d in turn_space...]
  transfers between devices with their start and end apart: 48 -> 31, of which waited for: 21 -> 12; matrix products, arithmetic and copies ran while one was open for 19% -> 5% of each run, Pallas kernels for 0% -> 19%
where the time goes in v1:
time: 646 us; the launch traced here: 634 us
  Pallas kernels  218 us (34%)
  waiting for transfers between devices  206 us (32%)
  starting transfers between devices  89.1 us (14%)
  blocking collectives  40.4 us (6%)
  local copies, waits for them, and re-layouts  36.4 us (6%)
  other arithmetic  27.7 us (4%)
  between operations  14.9 us (2%)
    all_gather x1, waiting for transfers between devices, fast_shards(): full = lax.all_gather(jnp.stack([packed, other]), CUBE, axis=0, tiled=False)  63.2 us
    all_to_all x4, waiting for transfers between devices, swap_frames(): lax.all_to_all(block.reshape(16, rows, block.shape[-1]), CUBE, 0, 0, tile...  53.1 us
    ppermute x2, waiting for transfers between devices, from_slot(): lax.ppermute(pick(1 - half, pieces), PAIR, [(d, s) for s, d in turn_space...  49.9 us
    all_to_all x4, starting transfers between devices, swap_frames(): lax.all_to_all(block.reshape(16, rows, block.shape[-1]), CUBE, 0, 0, tile...  33.8 us
    pallas_call x1, Pallas kernels, self_back_block(): kernel_call(self_back_kernel, [((PIX, C), SINGLE), (packed_shape(24), NAR...  28.4 us
    pallas_call x1, Pallas kernels, attn_block(): kernel_call(attn_kernel, [((PIX, 3 * C), NARROW), full, ((PIX, 8), SINGLE...  27.8 us
    pallas_call x1, Pallas kernels, time_back_block(): kernel_call(time_back_kernel, [((16, PIX // 16, 3 * C), NARROW), ((HEADS,...  26 us
    pallas_call x1, Pallas kernels, cross_back(): kernel_call(cross_back_kernel, [((PIX, C), SINGLE), (packed_shape(64), NA...  25 us
  transfers between devices with their start and end apart: 31, of which 12 were waited for; matrix products, arithmetic and copies ran while one was open for 5% of the time, Pallas kernels for 19%

profile of v1, /device:TPU:0, one launch (start us, length us, event | category | flops | bytes accessed | tf_op | source)
XLA Modules:
  0.0 633.7 jit_solution(16497009448612339754)
XLA Ops:
  16.5 15.8 %collective-permute-done = bf16[272,640]{1,0:T(8,128)(2,1)S(1)} collective-permute-done((bf16[272,640]{1,0:T(8,128)(2,1)}, bf16[272,640]{1,0:T(8,128)(2,1)S(1)}, u32[]{:S(2)}, u32[]{:S(2)}) %collective-permute-start) | collective-permute-done | bytes 348192 | tf_op jit(solution)/shard_map/ppermute | solution.py:1437
  37.8 63.2 %all-gather.3.cloned.1.call-done = bf16[32,272,640]{2,1,0:T(8,128)(2,1)} async-done(((bf16[2,272,640]{2,1,0:T(8,128)(2,1)}), bf16[32,272,640]{2,1,0:T(8,128)(2,1)}) %all-gather.3.cloned.1.call-update) | async-done | bytes 11141136 | tf_op jit(solution)/shard_map/all_gather | solution.py:1438
  111.4 11.2 %shard_map.343 = (bf16[2880,320]{1,0:T(8,128)(2,1)}, bf16[2880,320]{1,0:T(8,128)(2,1)}, bf16[1280,640]{1,0:T(8,128)(2,1)}, bf16[320,960]{1,0:T(8,128)(2,1)}, bf1...) custom-call(s32[1]{0:T(128)} %bitcast.2.half_ref, ...), custom_call_target="tpu_custom_call" | custom-call | flops 10000000000 | bytes 10000000 | tf_op jit(solution)/shard_map/pallas_call | solution.py:1334
  125.1 16.4 %shard_map.344 = (f32[1152,320]{1,0:T(8,128)}, f32[1152,320]{1,0:T(8,128)}, bf16[1248,960]{1,0:T(8,128)(2,1)}, bf16[1248,960]{1,0:T(8,128)(2,1)}, f32[8,320]{1,0:T(8,128)}, /*index=5*/f32[8,640]{1,0:T(8,128)}) custom-call(bf16[1152,320]{1,0:T(8,128)(2,1)} %pad_maximum_fusion.x_ref, bf16[2880,320]{1,0:T(8,128)(2,1)} %get-tuple-element.120.w1_ref, ...), custom_call_target="tpu_custom_call" | custom-call | flops 15000000512 | bytes 10000000 | tf_op jit(solution)/shard_map/pallas_call | solution.py:717
  141.4 27.8 %shard_map.345 = (bf16[1152,960]{1,0:T(8,128)(2,1)}, f32[1152,320]{1,0:T(8,128)}, f32[1152,8]{1,0:T(8,128)}, f32[1152,320]{1,0:T(8,128)}, bf16[128,640]{1,0:T(8,...) custom-call(f32[1152,320]{1,0:T(8,128)} %get-tuple-element.123.sec1_, ...), custom_call_target="tpu_custom_call" | custom-call | flops 28000000000 | bytes 10000000 | tf_op jit(solution)/shard_map/pallas_call | solution.py:787
  169.3 15.4 %all-to-all-start = ((bf16[16,72,960]{2,1,0:T(8,128)(2,1)}), bf16[16,72,960]{2,1,0:T(8,128)(2,1)}, u32[]{:S(2)}, u32[]{:S(2)}) async-start(bf16[16,72,960]{2,1,0:T(8,128)(2,1)} %bitcast.74), calls=%async_computation | async-start | bytes 4718592 | tf_op jit(solution)/shard_map/all_to_all | solution.py:1417
  196.8 18.1 %all-to-all-done.qkv_ref = bf16[16,72,960]{2,1,0:T(8,128)(2,1)} async-done(((bf16[16,72,960]{2,1,0:T(8,128)(2,1)}), bf16[16,72,960]{2,1,0:T(8,128)(2,1)}, u32[]{:S(2)}, u32[]{:S(2)}) %all-to-all-start) | async-done | bytes 2211872 | tf_op jit(solution)/shard_map/all_to_all | solution.py:1417
  214.9 15.1 %shard_map.346 = (bf16[16,72,320]{2,1,0:T(8,128)(2,1)}, f32[16,72,320]{2,1,0:T(8,128)}, f32[1152,8]{1,0:T(8,128)}) custom-call(bf16[16,72,960]{2,1,0:T(8,128)(2,1)} %all-to-all-done.qkv_ref, f32[5,128,128]{2,1,0:T(8,128)} %copy.74.bias_ref), custom_call_target="tpu_custom_call" | custom-call | flops 15000000512 | bytes 10000000 | tf_op jit(solution)/shard_map/pallas_call | solution.py:1001
  242.1 15.7 %collective-permute-done.8 = bf16[576,320]{1,0:T(8,128)(2,1)S(1)} collective-permute-done((bf16[576,320]{1,0:T(8,128)(2,1)S(1)}, bf16[576,320]{1,0:T(8,128)(2,1)S(1)}, u32[]{:S(2)}, u32[]{:S(2)}) %collective-permute-start.8) | collective-permute-done | bytes 368672 | tf_op jit(solution)/shard_map/ppermute | solution.py:549
  259.8 17.9 %shard_map.347 = (bf16[1152,320]{1,0:T(8,128)(2,1)}, f32[1152,320]{1,0:T(8,128)}, bf16[1152,320]{1,0:T(8,128)(2,1)}, bf16[2,8,2,48,640]{4,3,2,1,0:T(8,128)(2,1)}, f32[8,320]{1,0:T(8,128)}) custom-call(f32[1152,320]{1,0:T(8,128)} %get-tuple-element.131.sec3_ref, bf16[1152,320]{1,0:T(8,128)(2,1)} %bitcast.80, bf16[1152,320]{1,0:T(8,128)(2,1)} %pad_maximum_fusion.1.cot_ref, ...), custom_call_target="tpu_custom_call" | custom-call | flops 20000000000 | bytes 10000000 | tf_op jit(solution)/shard_map/pallas_call | solution.py:968
  277.8 7.7 %all-to-all-start.2 = ((bf16[16,72,320]{2,1,0:T(8,128)(2,1)}), bf16[16,72,320]{2,1,0:T(8,128)(2,1)S(1)}, u32[]{:S(2)}, u32[]{:S(2)}) async-start(bf16[16,72,320]{2,1,0:T(8,128)(2,1)} %bitcast.81), calls=%async_computation.2 | async-start | bytes 1769472 | tf_op jit(solution)/shard_map/all_to_all | solution.py:1417
  285.4 13.0 %all-to-all-done.2.grad_ref = bf16[16,72,320]{2,1,0:T(8,128)(2,1)S(1)} async-done(((bf16[16,72,320]{2,1,0:T(8,128)(2,1)}), bf16[16,72,320]{2,1,0:T(8,128)(2,1)S(1)}, u32[]{:S(2)}, u32[]{:S(2)}) %all-to-all-start.2) | async-done | bytes 737312 | tf_op jit(solution)/shard_map/all_to_all | solution.py:1417
  310.0 26.0 %shard_map.348 = (bf16[16,72,960]{2,1,0:T(8,128)(2,1)}, f32[5,128,128]{2,1,0:T(8,128)}) custom-call(bf16[16,72,960]{2,1,0:T(8,128)(2,1)} %all-to-all-done.qkv_ref, f32[5,128,128]{2,1,0:T(8,128)} %fusion.18.bias_ref, f32[16,72,320]{2,1,0:T(8,128)} %get-tuple-element.139.mix_ref, f32[1152,8]{1,0:T(8,128)} %get-tuple-element.140.lse_ref, ...), custom_call_target="tpu_custom_call" | custom-call | flops 24999999488 | bytes 10000000 | tf_op jit(solution)/shard_map/pallas_call | solution.py:1040
  350.6 21.9 %all-to-all-done.4 = bf16[16,72,960]{2,1,0:T(8,128)(2,1)S(1)} async-done(((bf16[16,72,960]{2,1,0:T(8,128)(2,1)}), bf16[16,72,960]{2,1,0:T(8,128)(2,1)S(1)}, u32[]{:S(2)}, u32[]{:S(2)}) %all-to-all-start.4) | async-done | bytes 2211872 | tf_op jit(solution)/shard_map/all_to_all | solution.py:1417
  378.8 25.0 %shard_map.349 = (f32[1152,320]{1,0:T(8,128)}, bf16[2,8,2,64,640]{4,3,2,1,0:T(8,128)(2,1)}, f32[8,320]{1,0:T(8,128)}) custom-call(f32[1152,320]{1,0:T(8,128)} %get-tuple-element.138.carried_ref, bf16[1152,960]{1,0:T(8,128)(2,1)} %bitcast.75, f32[1152,320]{1,0:T(8,128)} %get-tuple-element.131.sec3_ref, f32[1152,320]{1,0:T(8,128)} %get-tuple-element.153.sec2_ref, ...), custom_call_target="tpu_custom_call" | custom-call | flops 25999998976 | bytes 10000000 | tf_op jit(solution)/shard_map/pallas_call | solution.py:873
  403.8 13.1 %collective-permute-done.11 = bf16[576,320]{1,0:T(8,128)(2,1)S(1)} collective-permute-done((bf16[576,320]{1,0:T(8,128)(2,1)S(1)}, bf16[576,320]{1,0:T(8,128)(2,1)S(1)}, u32[]{:S(2)}, u32[]{:S(2)}) %collective-permute-start.11) | collective-permute-done | bytes 368672 | tf_op jit(solution)/shard_map/ppermute | solution.py:558
  426.6 28.4 %shard_map.350 = (f32[1152,320]{1,0:T(8,128)}, bf16[2,8,2,24,640]{4,3,2,1,0:T(8,128)(2,1)}, f32[8,320]{1,0:T(8,128)}) custom-call(f32[1152,320]{1,0:T(8,128)} %get-tuple-element.166.carried_ref, f32[1152,320]{1,0:T(8,128)} %get-tuple-element.123.sec1_ref, bf16[1152,960]{1,0:T(8,128)(2,1)} %get-tuple-element.167.proj_ref, ...), custom_call_target="tpu_custom_call" | custom-call | flops 28999999488 | bytes 10000000 | tf_op jit(solution)/shard_map/pallas_call | solution.py:924
  455.1 8.7 %shard_map.351 = (bf16[2,8,2,72,640]{4,3,2,1,0:T(8,128)(2,1)}, bf16[1152,320]{1,0:T(8,128)(2,1)}) custom-call(f32[1152,320]{1,0:T(8,128)} %get-tuple-element.170.carried_ref, bf16[1248,960]{1,0:T(8,128)(2,1)} %get-tuple-element.172.cols2_ref, bf16[2,8,2,24,640]{4,3,2,1,0:T(8,128)(2,1)} %get-tuple-element.173.upper_ref), custom_call_target="tpu_custom_call" | custom-call | flops 8999999488 | bytes 10000000 | tf_op jit(solution)/shard_map/pallas_call | solution.py:1092
  466.9 10.2 %shard_map.352 = (f32[1152,320]{1,0:T(8,128)}, bf16[1152,320]{1,0:T(8,128)(2,1)}, f32[8,320]{1,0:T(8,128)}) custom-call(bf16[1152,320]{1,0:T(8,128)(2,1)} %get-tuple-element.177.back_s, f32[1152,320]{1,0:T(8,128)} %get-tuple-element.178.conv_out_ref, f32[8,320]{1,0:T(8,128)} %get-tuple-element.171.stats_ref, f32[8,640]{1,0:T(8,128)} %get-tuple-element.179.film_ref, ...), custom_call_target="tpu_custom_call" | custom-call | flops 8999999488 | bytes 10000000 | tf_op jit(solution)/shard_map/pallas_call | solution.py:1134
  477.7 7.5 %shard_map.353 = bf16[2,8,2,48,640]{4,3,2,1,0:T(8,128)(2,1)} custom-call(bf16[1248,960]{1,0:T(8,128)(2,1)} %get-tuple-element.184.cols1_ref, bf16[1152,320]{1,0:T(8,128)(2,1)} %get-tuple-element.185.back_ref), custom_call_target="tpu_custom_call" | custom-call | flops 8999999488 | bytes 10000000 | tf_op jit(solution)/shard_map/pallas_call | solution.py:1148
  495.5 9.7 %shard_map.354 = (bf16[1152,320]{1,0:T(8,128)(2,1)}, f32[8,320]{1,0:T(8,128)}) custom-call(f32[1152,320]{1,0:T(8,128)} %get-tuple-element.170.carried_ref, bf16[1152,320]{1,0:T(8,128)(2,1)} %pad_maximum_fusion.x_ref, f32[8,320]{1,0:T(8,128)} %get-tuple-element.171.stats_ref, f32[6,320]{1,0:T(8,128)} %bitcast.100, f32[320,320]{1,0:T(8,128)} %compare_convert_fusion.gmat_ref, ...), custom_call_target="tpu_custom_call" | custom-call | flops 11000000512 | bytes 10000000 | tf_op jit(solution)/shard_map/pallas_call | solution.py:1247
  506.1 16.8 %all_to_all.45.got_ref = f32[16,16,640]{2,1,0:T(8,128)} all-to-all(f32[16,16,640]{2,1,0:T(8,128)S(1)} %maximum_maximum_fusion), channel_id=1, replica_groups=mesh['half'=2,'quad'=4,'core'=2,'space'=2] {'quad','core','space'}, dimensions={0} | all-to-all | bytes 1310720 | tf_op jit(solution)/shard_map/all_to_all | solution.py:1182
  522.9 23.5 %all_to_all.46.got_ref = bf16[8,2,72,640]{3,2,1,0:T(8,128)(2,1)} all-to-all(bf16[8,2,72,640]{3,2,1,0:T(8,128)(2,1)S(1)} %fusion), channel_id=1, replica_groups=mesh['half'=2,'quad'=4,'core'=2,'space'=2] {'quad','space'}, dimensions={0} | all-to-all | bytes 2949120 | tf_op jit(solution)/shard_map/all_to_all | solution.py:1390
  564.0 36.8 %collective-permute-done.16 = bf16[576,320]{1,0:T(8,128)(2,1)S(1)} collective-permute-done((bf16[576,320]{1,0:T(8,128)(2,1)S(1)}, bf16[576,320]{1,0:T(8,128)(2,1)S(1)}, u32[]{:S(2)}, u32[]{:S(2)}) %collective-permute-start.16) | collective-permute-done | bytes 368672 | tf_op jit(solution)/shard_map/ppermute | solution.py:558
  (220 shorter events, 154.0 us)
Async XLA Ops:
  7.2 93.8 %all-gather.3.cloned.1.call-start = ((), (), s32[]{:S(2)}) async-start(), calls=%async_computation.9 | async-start | bytes 11837440 | tf_op jit(solution)/shard_map/all_gather | solution.py:1438
  12.4 19.9 %collective-permute-start = (bf16[272,640]{1,0:T(8,128)(2,1)}, bf16[272,640]{1,0:T(8,128)(2,1)S(1)}, u32[]{:S(2)}, u32[]{:S(2)}) collective-permute-start(bf16[272,640]{1,0:T(8,128)(2,1)} %shard_map.342), channel_id=1, source_target_pairs={{0,16},{16,0},{1,17},{17,1},{2,18},{18,2},{3,19},{19,3},{4,20},{20... | collective-permute-start | bytes 1044488 | tf_op jit(solution)/shard_map/ppermute | solution.py:1437
  101.2 22.2 %collective-permute-start.1 = (bf16[576,320]{1,0:T(8,128)(2,1)S(1)}, bf16[576,320]{1,0:T(8,128)(2,1)S(1)}, u32[]{:S(2)}, u32[]{:S(2)}) collective-permute-start(bf16[576,320]{1,0:T(8,128)(2,1)S(1)} %bitcast.85), channel_id=1, source_target_pairs={{0,0},{1,16},{16,1},{17,17},{2,2},{3,18},{18,3},{19,19},{4,4},{5,2... | collective-permute-start | bytes 1105928 | tf_op jit(solution)/shard_map/ppermute | solution.py:548
  101.9 21.5 %collective-permute-start.2 = (bf16[576,320]{1,0:T(8,128)(2,1)S(1)}, bf16[576,320]{1,0:T(8,128)(2,1)S(1)}, u32[]{:S(2)}, u32[]{:S(2)}) collective-permute-start(bf16[576,320]{1,0:T(8,128)(2,1)S(1)} %bitcast.84), channel_id=1, source_target_pairs={{0,16},{1,0},{16,17},{17,1},{2,18},{3,2},{18,19},{19,3},{4,20},{5,... | collective-permute-start | bytes 1105928 | tf_op jit(solution)/shard_map/ppermute | solution.py:549
  105.8 16.7 %collective-permute-start.4 = (bf16[64,1024]{1,0:T(8,128)(2,1)S(1)}, bf16[64,1024]{1,0:T(8,128)(2,1)S(1)}, u32[]{:S(2)}, u32[]{:S(2)}) collective-permute-start(bf16[64,1024]{1,0:T(8,128)(2,1)S(1)} %get-tuple-element.288), channel_id=1, source_target_pairs={{0,0},{1,16},{16,1},{17,17},{2,2},{3,18},{18,3},{19,19},{4,4},{5,2... | collective-permute-start | bytes 393224 | tf_op jit(solution)/shard_map/ppermute | solution.py:548
  106.5 16.1 %collective-permute-start.5 = (bf16[64,1024]{1,0:T(8,128)(2,1)S(1)}, bf16[64,1024]{1,0:T(8,128)(2,1)S(1)}, u32[]{:S(2)}, u32[]{:S(2)}) collective-permute-start(bf16[64,1024]{1,0:T(8,128)(2,1)S(1)} %get-tuple-element.289), channel_id=1, source_target_pairs={{0,16},{1,0},{16,17},{17,1},{2,18},{3,2},{18,19},{19,3},{4,20},{5,... | collective-permute-start | bytes 393224 | tf_op jit(solution)/shard_map/ppermute | solution.py:549
  169.3 45.7 %all-to-all-start = ((bf16[16,72,960]{2,1,0:T(8,128)(2,1)}), bf16[16,72,960]{2,1,0:T(8,128)(2,1)}, u32[]{:S(2)}, u32[]{:S(2)}) async-start(bf16[16,72,960]{2,1,0:T(8,128)(2,1)} %bitcast.74), calls=%async_computation | async-start | bytes 4718592 | tf_op jit(solution)/shard_map/all_to_all | solution.py:1417
  230.0 28.9 %all-to-all-start.1 = ((bf16[16,72,320]{2,1,0:T(8,128)(2,1)}), bf16[16,72,320]{2,1,0:T(8,128)(2,1)S(1)}, u32[]{:S(2)}, u32[]{:S(2)}) async-start(bf16[16,72,320]{2,1,0:T(8,128)(2,1)} %get-tuple-element.133), calls=%async_computation.1 | async-start | bytes 1769472 | tf_op jit(solution)/shard_map/all_to_all | solution.py:1417
  235.7 6.4 %collective-permute-start.7 = (bf16[576,320]{1,0:T(8,128)(2,1)S(1)}, bf16[576,320]{1,0:T(8,128)(2,1)S(1)}, u32[]{:S(2)}, u32[]{:S(2)}) collective-permute-start(bf16[576,320]{1,0:T(8,128)(2,1)S(1)} %bitcast.83), channel_id=1, source_target_pairs={{0,0},{1,16},{16,1},{17,17},{2,2},{3,18},{18,3},{19,19},{4,4},{5,2... | collective-permute-start | bytes 1105928 | tf_op jit(solution)/shard_map/ppermute | solution.py:548
  236.4 21.4 %collective-permute-start.8 = (bf16[576,320]{1,0:T(8,128)(2,1)S(1)}, bf16[576,320]{1,0:T(8,128)(2,1)S(1)}, u32[]{:S(2)}, u32[]{:S(2)}) collective-permute-start(bf16[576,320]{1,0:T(8,128)(2,1)S(1)} %bitcast.82), channel_id=1, source_target_pairs={{0,16},{1,0},{16,17},{17,1},{2,18},{3,2},{18,19},{19,3},{4,20},{5,... | collective-permute-start | bytes 1105928 | tf_op jit(solution)/shard_map/ppermute | solution.py:549
  277.8 20.7 %all-to-all-start.2 = ((bf16[16,72,320]{2,1,0:T(8,128)(2,1)}), bf16[16,72,320]{2,1,0:T(8,128)(2,1)S(1)}, u32[]{:S(2)}, u32[]{:S(2)}) async-start(bf16[16,72,320]{2,1,0:T(8,128)(2,1)} %bitcast.81), calls=%async_computation.2 | async-start | bytes 1769472 | tf_op jit(solution)/shard_map/all_to_all | solution.py:1417
  306.4 29.5 %all-to-all-start.3 = ((bf16[8,2,48,640]{3,2,1,0:T(8,128)(2,1)}), bf16[8,2,48,640]{3,2,1,0:T(8,128)(2,1)S(1)}, u32[]{:S(2)}, u32[]{:S(2)}) async-start(bf16[8,2,48,640]{3,2,1,0:T(8,128)(2,1)} %fusion.3), calls=%async_computation.3 | async-start | bytes 1966080 | tf_op jit(solution)/shard_map/all_to_all | solution.py:1390
  336.9 35.5 %all-to-all-start.4 = ((bf16[16,72,960]{2,1,0:T(8,128)(2,1)}), bf16[16,72,960]{2,1,0:T(8,128)(2,1)S(1)}, u32[]{:S(2)}, u32[]{:S(2)}) async-start(bf16[16,72,960]{2,1,0:T(8,128)(2,1)} %get-tuple-element.149), calls=%async_computation.4 | async-start | bytes 4718592 | tf_op jit(solution)/shard_map/all_to_all | solution.py:1417
  372.6 31.2 %collective-permute-start.10 = (bf16[576,320]{1,0:T(8,128)(2,1)S(1)}, bf16[576,320]{1,0:T(8,128)(2,1)S(1)}, u32[]{:S(2)}, u32[]{:S(2)}) collective-permute-start(bf16[576,320]{1,0:T(8,128)(2,1)S(1)} %get-tuple-element.276), channel_id=1, source_target_pairs={{0,0},{16,1},{1,16},{17,17},{2,2},{18,3},{3,18},{19,19},{4,4},{20,... | collective-permute-start | bytes 1105928 | tf_op jit(solution)/shard_map/ppermute | solution.py:557
  373.3 43.6 %collective-permute-start.11 = (bf16[576,320]{1,0:T(8,128)(2,1)S(1)}, bf16[576,320]{1,0:T(8,128)(2,1)S(1)}, u32[]{:S(2)}, u32[]{:S(2)}) collective-permute-start(bf16[576,320]{1,0:T(8,128)(2,1)S(1)} %get-tuple-element.277), channel_id=1, source_target_pairs={{16,0},{0,1},{17,16},{1,17},{18,2},{2,3},{19,18},{3,19},{20,4},{4,... | collective-permute-start | bytes 1105928 | tf_op jit(solution)/shard_map/ppermute | solution.py:558
  423.0 40.7 %all-to-all-start.5 = ((bf16[8,2,64,640]{3,2,1,0:T(8,128)(2,1)}), bf16[8,2,64,640]{3,2,1,0:T(8,128)(2,1)S(1)}, u32[]{:S(2)}, u32[]{:S(2)}) async-start(bf16[8,2,64,640]{3,2,1,0:T(8,128)(2,1)} %fusion.1), calls=%async_computation.5 | async-start | bytes 2621440 | tf_op jit(solution)/shard_map/all_to_all | solution.py:1390
  466.8 10.3 %collective-permute-start.13 = (bf16[8,2,72,640]{3,2,1,0:T(8,128)(2,1)S(1)}, bf16[8,2,72,640]{3,2,1,0:T(8,128)(2,1)S(1)}, u32[]{:S(2)}, u32[]{:S(2)}) collective-permute-start(bf16[8,2,72,640]{3,2,1,0:T(8,128)(2,1)S(1)} %select_bitcast_fusion), channel_id=1, source_target_pairs={{0,2},{2,0},{1,3},{3,1},{4,6},{6,4},{5,7},{7,5},{8,10},{10,8},{9,1... | collective-permute-start | bytes 4423688 | tf_op jit(solution)/shard_map/ppermute | solution.py:1385
  546.5 65.6 %all-to-all-start.8 = ((bf16[8,2,48,640]{3,2,1,0:T(8,128)(2,1)}), bf16[8,2,48,640]{3,2,1,0:T(8,128)(2,1)S(1)}, u32[]{:S(2)}, u32[]{:S(2)}) async-start(bf16[8,2,48,640]{3,2,1,0:T(8,128)(2,1)} %fusion.2), calls=%async_computation.8 | async-start | bytes 1966080 | tf_op jit(solution)/shard_map/all_to_all | solution.py:1390
  550.2 13.8 %collective-permute-start.15 = (bf16[576,320]{1,0:T(8,128)(2,1)S(1)}, bf16[576,320]{1,0:T(8,128)(2,1)S(1)}, u32[]{:S(2)}, u32[]{:S(2)}) collective-permute-start(bf16[576,320]{1,0:T(8,128)(2,1)S(1)} %get-tuple-element.272), channel_id=1, source_target_pairs={{0,0},{16,1},{1,16},{17,17},{2,2},{18,3},{3,18},{19,19},{4,4},{20,... | collective-permute-start | bytes 1105928 | tf_op jit(solution)/shard_map/ppermute | solution.py:557
  550.9 49.9 %collective-permute-start.16 = (bf16[576,320]{1,0:T(8,128)(2,1)S(1)}, bf16[576,320]{1,0:T(8,128)(2,1)S(1)}, u32[]{:S(2)}, u32[]{:S(2)}) collective-permute-start(bf16[576,320]{1,0:T(8,128)(2,1)S(1)} %get-tuple-element.273), channel_id=1, source_target_pairs={{16,0},{0,1},{17,16},{1,17},{18,2},{2,3},{19,18},{3,19},{20,4},{4,... | collective-permute-start | bytes 1105928 | tf_op jit(solution)/shard_map/ppermute | solution.py:558
  558.9 59.8 %collective-permute-start.18 = (bf16[48,640]{1,0:T(8,128)(2,1)}, bf16[48,640]{1,0:T(8,128)(2,1)S(1)}, u32[]{:S(2)}, u32[]{:S(2)}) collective-permute-start(bf16[48,640]{1,0:T(8,128)(2,1)} %get-tuple-element.196), channel_id=1, source_target_pairs={{0,16},{16,0},{1,17},{17,1},{2,18},{18,2},{3,19},{19,3},{4,20},{20... | collective-permute-start | bytes 184328 | tf_op jit(solution)/shard_map/ppermute | solution.py:1396
  561.0 57.7 %collective-permute-start.19 = (bf16[64,640]{1,0:T(8,128)(2,1)}, bf16[64,640]{1,0:T(8,128)(2,1)S(1)}, u32[]{:S(2)}, u32[]{:S(2)}) collective-permute-start(bf16[64,640]{1,0:T(8,128)(2,1)} %get-tuple-element.199), channel_id=1, source_target_pairs={{0,16},{16,0},{1,17},{17,1},{2,18},{18,2},{3,19},{19,3},{4,20},{20... | collective-permute-start | bytes 245768 | tf_op jit(solution)/shard_map/ppermute | solution.py:1396
  604.1 14.6 %collective-permute-start.22 = (bf16[80,320]{1,0:T(8,128)(2,1)S(1)}, bf16[80,320]{1,0:T(8,128)(2,1)S(1)}, u32[]{:S(2)}, u32[]{:S(2)}) collective-permute-start(bf16[80,320]{1,0:T(8,128)(2,1)S(1)} %copy-done.30), channel_id=1, source_target_pairs={{0,16},{16,0},{1,17},{17,1},{2,18},{18,2},{3,19},{19,3},{4,20},{20... | collective-permute-start | bytes 153608 | tf_op jit(solution)/shard_map/ppermute | solution.py:1187
  612.1 6.7 %collective-permute-start.20 = (bf16[72,640]{1,0:T(8,128)(2,1)}, bf16[72,640]{1,0:T(8,128)(2,1)S(1)}, u32[]{:S(2)}, u32[]{:S(2)}) collective-permute-start(bf16[72,640]{1,0:T(8,128)(2,1)} %get-tuple-element.202), channel_id=1, source_target_pairs={{0,16},{16,0},{1,17},{17,1},{2,18},{18,2},{3,19},{19,3},{4,20},{20... | collective-permute-start | bytes 276488 | tf_op jit(solution)/shard_map/ppermute | solution.py:1396
  (40 other events, 639.0 us)
Sparse Core Ops, SparseCore 0:
  34.4 66.5 all-gather.2
